TPU v7x, 128 devices: a whole 4x4x4 slice. The times are simulated.
128 devices in a mesh: row: 8 (over x_hi, y), col: 16 (over x_lo, z, core).
Axes of the slice: x: 4 (x_hi: 2, x_lo: 2; x = x_hi * 2 + x_lo), y: 4, z: 4, core: 2. Of those that a mesh axis runs over, the one named last changes fastest.
Arguments:
- tokens: bfloat16 [16384, 768], P(('row', 'col')), may hold values from -6 to 6
- expert_ids: int32 [16384, 2], P(('row', 'col')), may hold values from 0 to 31, all different within a row; in each aligned block of 128 rows (0 to 127, 128 to 255, ...) at most 16 rows name the same one
- text: bfloat16 [1024, 768], P(('row', 'col')), may hold values from -6 to 6
- w_gate: bfloat16 [32, 768, 3072], P('col', None, 'row'), may hold values from -0.21875 to 0.21875
- w_up: bfloat16 [32, 768, 3072], P('col', None, 'row'), may hold values from -0.21875 to 0.21875
- w_down: bfloat16 [32, 3072, 768], P('col', 'row'), may hold values from -0.109375 to 0.109375
- router: float32 [768, 32], replicated, may hold values from -0.21875 to 0.21875
- log_scale: float32 [1], replicated, may hold values from 1 to 2.3
- bias: float32 [1], replicated, may hold values from -1 to 0.5
- loss_scale: float32 [1], replicated, may hold values from 32768 to 524288
Outputs:
- d_text: float32 [1024, 768], P(('row', 'col'))
- d_tokens: float32 [16384, 768], P(('row', 'col'))
- d_gate: float32 [32, 768, 3072], P('col', None, 'row')
- d_up: float32 [32, 768, 3072], P('col', None, 'row')
- d_down: float32 [32, 3072, 768], P('col', 'row')
- d_router: float32 [768, 32], replicated
Inputs may be any that keep to these rules, and one draw needn't show every extreme that they name: `expert_ids`: the two ids of a token differ. Among the 128 rows of one device no expert is named more than 16 times, a bound that some block reaches.
All inputs are finite; a program needn't handle non-finite values.
Results may differ from a plain program's by a relative error of at most 0.025.
Values may be sent and summed in bfloat16 or wider, within the bound.
A program may use at most 128 MiB of HBM per device.

v0:
```python
import jax
import jax.numpy as jnp
from jax import lax
from jax.sharding import PartitionSpec as P

EXP_DEV = 2
SEQ = 16


def spread(buffer):
    arrived = lax.all_to_all(buffer, "col", split_axis=0, concat_axis=0, tiled=True)
    return lax.all_gather(arrived, "row", axis=0, tiled=True)


def collect(partial_out):
    summed = lax.psum_scatter(
        partial_out.astype(jnp.bfloat16), "row", scatter_dimension=0, tiled=True
    )
    returned = lax.all_to_all(summed, "col", split_axis=0, concat_axis=0, tiled=True)
    return returned.reshape(-1, partial_out.shape[-1])


def pair_block(embed_b, text_block, own_rows, text_rows, scale, shift, factor):
    logits = (
        scale * jnp.einsum("sd,td->st", embed_b, text_block, preferred_element_type=jnp.float32)
        + shift
    )
    labels = jnp.where(own_rows[:, None] == text_rows[None, :], 1.0, -1.0).astype(jnp.float32)
    return (-factor * labels * jax.nn.sigmoid(-labels * logits)).astype(jnp.bfloat16)


def body(tokens, expert_ids, text, w_gate, w_up, w_down, router, log_scale, bias, loss_scale):
    n_row = lax.axis_size("row")
    n_col = lax.axis_size("col")
    tok_count = tokens.shape[0]
    width = tokens.shape[1]
    samples = tok_count // SEQ
    experts = EXP_DEV * n_col
    capacity = max(2, 4 * tok_count // experts)
    batch = samples * n_row * n_col
    token_wide = tokens.astype(jnp.float32)
    inverse_rms = lax.rsqrt(jnp.mean(token_wide * token_wide, -1, keepdims=True) + 1e-06)
    normed = token_wide * inverse_rms
    norm_in = normed.astype(jnp.bfloat16)
    norm_wide = norm_in.astype(jnp.float32)
    scores = jnp.dot(norm_wide, router, precision=lax.Precision.HIGHEST)
    choose = (expert_ids[:, :, None] == jnp.arange(experts, dtype=jnp.int32)[None, None, :]).astype(
        jnp.float32
    )
    chosen = jnp.sum(choose * scores[:, None, :], -1)
    gates = jax.nn.sigmoid(chosen - chosen[:, ::-1])
    flat_expert = expert_ids.reshape(-1)
    member = (flat_expert[:, None] == jnp.arange(experts, dtype=jnp.int32)[None, :]).astype(
        jnp.int32
    )
    position = jnp.sum(jnp.cumsum(member, 0) * member, 1) - 1
    slot_index = flat_expert * capacity + position
    table = (
        slot_index[None, :] == jnp.arange(experts * capacity, dtype=jnp.int32)[:, None]
    ).astype(jnp.bfloat16)
    pair_rows = jnp.repeat(norm_in, 2, axis=0)
    outgoing = jnp.dot(table, pair_rows, preferred_element_type=jnp.float32).astype(jnp.bfloat16)
    grid = spread(outgoing.reshape(n_col, EXP_DEV, capacity, width))
    gate_pre = jnp.einsum("sxcd,xdf->sxcf", grid, w_gate, preferred_element_type=jnp.float32)
    up_pre = jnp.einsum("sxcd,xdf->sxcf", grid, w_up, preferred_element_type=jnp.float32)
    sigma = jax.nn.sigmoid(gate_pre)
    silu_gate = gate_pre * sigma
    hidden = (silu_gate * up_pre).astype(jnp.bfloat16)
    y_slots = collect(
        jnp.einsum("sxcf,xfd->sxcd", hidden, w_down, preferred_element_type=jnp.float32)
    )
    y_pairs = jnp.dot(table.T, y_slots, preferred_element_type=jnp.float32).reshape(
        tok_count, 2, width
    )
    moe_out = token_wide + gates[:, 0, None] * y_pairs[:, 0] + gates[:, 1, None] * y_pairs[:, 1]
    pooled = jnp.mean(moe_out.reshape(samples, SEQ, width), 1)
    pooled_norm = jnp.sqrt(jnp.sum(pooled * pooled, -1, keepdims=True) + 1e-06)
    embed = pooled / pooled_norm
    embed_b = embed.astype(jnp.bfloat16)
    text_wide = text.astype(jnp.float32)
    text_norm = jnp.sqrt(jnp.sum(text_wide * text_wide, -1, keepdims=True) + 1e-06)
    text_unit = text_wide / text_norm
    text_b = text_unit.astype(jnp.bfloat16)
    scale = jnp.exp(log_scale[0])
    shift = bias[0]
    factor = loss_scale[0] * scale / batch
    own_rows = lax.axis_index(("row", "col")) * samples + jnp.arange(samples, dtype=jnp.int32)
    everyone = lax.all_gather(text_b, ("row", "col"), axis=0, tiled=True)
    weights = pair_block(
        embed_b, everyone, own_rows, jnp.arange(batch, dtype=jnp.int32), scale, shift, factor
    )
    embed_grad = jnp.dot(weights, everyone, preferred_element_type=jnp.float32)
    text_grad = lax.psum_scatter(
        jnp.einsum("st,sd->td", weights, embed_b, preferred_element_type=jnp.float32),
        ("row", "col"),
        scatter_dimension=0,
        tiled=True,
    )
    d_text = (text_grad - text_unit * jnp.sum(text_unit * text_grad, -1, keepdims=True)) / text_norm
    pooled_grad = (
        embed_grad - embed * jnp.sum(embed * embed_grad, -1, keepdims=True)
    ) / pooled_norm
    out_grad = jnp.repeat(pooled_grad / SEQ, SEQ, axis=0)
    gate_grad = jnp.sum(out_grad[:, None, :] * y_pairs, -1)
    down_in = (
        (gates[:, :, None] * out_grad[:, None, :])
        .astype(jnp.bfloat16)
        .reshape(2 * tok_count, width)
    )
    down_slots = jnp.dot(table, down_in, preferred_element_type=jnp.float32).astype(jnp.bfloat16)
    down_grid = spread(down_slots.reshape(n_col, EXP_DEV, capacity, width))
    hidden_grad = jnp.einsum(
        "sxcd,xfd->sxcf", down_grid, w_down, preferred_element_type=jnp.float32
    )
    slope = sigma * (1.0 + gate_pre * (1.0 - sigma))
    gate_delta = (hidden_grad * up_pre * slope).astype(jnp.bfloat16)
    up_delta = (hidden_grad * silu_gate).astype(jnp.bfloat16)
    d_down = jnp.einsum("sxcf,sxcd->xfd", hidden, down_grid, preferred_element_type=jnp.float32)
    d_gate = jnp.einsum("sxcd,sxcf->xdf", grid, gate_delta, preferred_element_type=jnp.float32)
    d_up = jnp.einsum("sxcd,sxcf->xdf", grid, up_delta, preferred_element_type=jnp.float32)
    input_part = jnp.einsum(
        "sxcf,xdf->sxcd", gate_delta, w_gate, preferred_element_type=jnp.float32
    ) + jnp.einsum("sxcf,xdf->sxcd", up_delta, w_up, preferred_element_type=jnp.float32)
    input_slots = collect(input_part)
    input_pairs = jnp.dot(table.T, input_slots, preferred_element_type=jnp.float32).reshape(
        tok_count, 2, width
    )
    logit_grad = gates * (gate_grad - jnp.sum(gates * gate_grad, -1, keepdims=True))
    score_grad = jnp.sum(logit_grad[:, :, None] * choose, 1)
    d_router = lax.psum(
        jnp.dot(norm_wide.T, score_grad, precision=lax.Precision.HIGHEST), ("row", "col")
    )
    norm_grad = (
        input_pairs[:, 0]
        + input_pairs[:, 1]
        + jnp.dot(score_grad, router.T, precision=lax.Precision.HIGHEST)
    )
    d_tokens = out_grad + inverse_rms * (
        norm_grad - normed * jnp.mean(norm_grad * normed, -1, keepdims=True)
    )
    return (d_text, d_tokens, d_gate, d_up, d_down, d_router)


def solution(mesh):
    in_specs = (
        P(("row", "col"), None),
        P(("row", "col"), None),
        P(("row", "col"), None),
        P("col", None, "row"),
        P("col", None, "row"),
        P("col", "row", None),
        P(),
        P(),
        P(),
        P(),
    )
    out_specs = (
        P(("row", "col"), None),
        P(("row", "col"), None),
        P("col", None, "row"),
        P("col", None, "row"),
        P("col", "row", None),
        P(),
    )
    return jax.shard_map(body, mesh=mesh, in_specs=in_specs, out_specs=out_specs, check_vma=False)
```

profile of v0, /device:TPU:1, one launch (start us, length us, event | category | flops | bytes accessed | tf_op | source)
XLA Modules:
  0.0 1322.9 jit_solution(1022894569984594867)
XLA Ops:
  8.1 0.9 copy.79
  8.9 0.1 reshape.131
  9.1 0.1 eq.93
  9.2 1.1 fusion.40
  10.3 0.6 reduce-window.6
  10.9 0.2 slice_reduce_fusion
  11.1 0.1 fusion.51
  11.2 1.0 fusion.30
  12.3 0.2 broadcast_in_dim.12
  12.5 0.1 reshape.133
  12.6 0.4 convolution_convert_fusion.1
  13.0 20.3 %all_to_all.20 = bf16[16,2,16,768]{3,2,1,0:T(8,128)(2,1)S(1)} all-to-all(bf16[16,2,16,768]{3,2,1,0:T(8,128)(2,1)S(1)} %bitcast.166), channel_id=1, replica_groups=mesh['row'=8,'col'=16] {'col'}, dimensions={0} | all-to-all | bytes 1572864 | tf_op jit(solution)/shard_map/all_to_all | solution.py:11
  33.3 1.3 copy.83
  34.8 87.8 %all-gather.4.cloned.1.call-done = bf16[128,2,16,768]{3,0,2,1:T(8,128)(2,1)} async-done(((bf16[16,2,16,768]{3,0,2,1:T(8,128)(2,1)}), bf16[128,2,16,768]{3,0,2,1:T(8,128)(2,1)}) %all-gather.4.cloned.1.call-update) | async-done | bytes 6291472 | tf_op jit(solution)/shard_map/all_gather | solution.py:12
  122.6 6.0 fusion.15
  128.6 5.7 fusion.4
  134.3 1.8 copy-done.11
  136.0 5.3 convert_bitcast_fusion
  141.4 0.6 copy-done.7
  142.0 0.1 fusion.53
  142.1 0.7 fusion.57
  144.8 0.1 sub.31
  145.0 0.3 fusion.58
  145.4 93.0 %reduce-scatter.4.cloned.1.call-done = bf16[16,2,16,768]{3,0,2,1:T(8,128)(2,1)} async-done(((bf16[128,2,16,768]{3,0,2,1:T(8,128)(2,1)}), bf16[16,2,16,768]{3,0,2,1:T(8,128)(2,1)}) %reduce-scatter.4.cloned.1.call-update) | async-done | bytes 786448 | tf_op jit(solution)/shard_map/reduce_scatter | solution.py:16
  238.4 2.2 copy.84
  240.6 5.7 all-to-all-start.1
  246.4 0.1 copy.85
  246.5 0.1 mul.223
  246.7 13.1 all-to-all-done.1
  259.7 0.9 copy-done.4
  260.6 1.5 fusion.34
  262.2 0.2 bitcast_reduce_fusion
  262.4 0.1 multiply_reduce_fusion.3
  262.5 109.2 %all-gather.6.cloned.1.call-done = bf16[1024,768]{1,0:T(8,128)(2,1)} async-done(((bf16[8,768]{1,0:T(8,128)(2,1)}), bf16[1024,768]{1,0:T(8,128)(2,1)}) %all-gather.6.cloned.1.call-update) | async-done | bytes 1572880 | tf_op jit(solution)/shard_map/all_gather | solution.py:88
  371.7 1.9 fusion.27
  373.6 1.8 multiply_reduce_fusion.1
  375.5 0.1 divide_multiply_fusion
  375.6 1.1 mul.225.clone
  376.8 2.6 mul.226
  379.3 1.6 convolution_convert_fusion
  380.9 17.1 %all_to_all.21 = bf16[16,2,16,768]{3,2,1,0:T(8,128)(2,1)S(1)} all-to-all(bf16[16,2,16,768]{3,2,1,0:T(8,128)(2,1)S(1)} %bitcast.163), channel_id=1, replica_groups=mesh['row'=8,'col'=16] {'col'}, dimensions={0} | all-to-all | bytes 1572864 | tf_op jit(solution)/shard_map/all_to_all | solution.py:11
  398.0 1.3 copy.87
  399.4 2.4 fusion.54
  401.8 0.2 reduce-scatter.8.cloned.1.call-start
  402.0 83.3 %all-gather.8.cloned.1.call-done = bf16[128,2,16,768]{3,0,2,1:T(8,128)(2,1)} async-done(((bf16[16,2,16,768]{3,0,2,1:T(8,128)(2,1)}), bf16[128,2,16,768]{3,0,2,1:T(8,128)(2,1)}) %all-gather.8.cloned.1.call-update) | async-done | bytes 6291472 | tf_op jit(solution)/shard_map/all_gather | solution.py:12
  485.3 13.3 %fusion.3 = (bf16[128,2,16,384]{3,0,2,1:T(8,128)(2,1)}, bf16[128,2,16,384]{3,0,2,1:T(8,128)(2,1)}) fusion(f32[2,128,16,384]{3,1,2,0:T(8,128)} %copy-done.10, f32[2,128,16,384]{3,1,2,0:T(8,128)} %get-tuple-element.13, bf16[128,2,16,768]{3,0,2,1:T(8,128)(2,1)} %all-gather.8.cloned.1.call-done, bf16[2,384,768]{2,1,0:T(8,128)(2,1)S(1)} %copy-done), kind=kOutput, calls=%fused_computation.6 | convolution fusion | flops 2436366336 | bytes 26345472 | tf_op jit(solution)/shard_map/sxcd,xfd->sxcf/dot_general | solution.py:112
  498.6 5.7 fusion.13
  504.3 8.3 fusion
  512.8 0.1 multiply_reduce_fusion
  512.9 0.8 fusion.59
  513.8 554.4 %reduce-scatter.6.cloned.1.call-done = f32[8,768]{1,0:T(8,128)} async-done(((f32[1024,768]{1,0:T(8,128)}), f32[8,768]{1,0:T(8,128)}) %reduce-scatter.6.cloned.1.call-update) | async-done | bytes 24592 | tf_op jit(solution)/shard_map/reduce_scatter | solution.py:93
  1068.2 0.9 multiply_reduce_fusion.2
  1069.1 1.4 subtract_divide_fusion
  1070.5 7.8 convolution_bitcast_fusion
  1078.4 91.6 %reduce-scatter.8.cloned.1.call-done = bf16[16,2,16,768]{3,0,2,1:T(8,128)(2,1)} async-done(((bf16[128,2,16,768]{3,0,2,1:T(8,128)(2,1)}), bf16[16,2,16,768]{3,0,2,1:T(8,128)(2,1)}) %reduce-scatter.8.cloned.1.call-update) | async-done | bytes 786448 | tf_op jit(solution)/shard_map/reduce_scatter | solution.py:16
  1170.0 2.3 copy.88
  1172.2 5.8 all-to-all-start.3
  1178.1 8.7 convolution_bitcast_fusion.1
  1186.8 7.7 convolution_bitcast_fusion.2
  1194.5 0.4 fusion.32
  1195.0 0.6 fusion.36
  1195.6 0.9 fusion.39
  1196.5 117.5 %all-reduce.2.cloned.1.call-done = f32[768,32]{0,1:T(8,128)} async-done(((f32[768,32]{0,1:T(8,128)}), f32[768,32]{0,1:T(8,128)}) %all-reduce.2.cloned.1.call-update) | async-done | bytes 98320 | tf_op jit(solution)/shard_map/psum | solution.py:130
  1314.0 1.5 copy.105
  (54 shorter events, 0.7 us)
Async XLA Ops:
  8.0 128.0 %copy-start = (bf16[2,384,768]{2,1,0:T(8,128)(2,1)S(1)}, bf16[2,384,768]{2,1,0:T(8,128)(2,1)}, u32[]{:S(2)}) copy-start(bf16[2,384,768]{2,1,0:T(8,128)(2,1)} %param.15) | copy-start | bytes 3538948
  8.0 114.5 %all-gather.4.cloned.1.call-start = ((), (), s32[]{:S(2)}) async-start(), calls=%async_computation.7 | async-start | bytes 7077888 | tf_op jit(solution)/shard_map/all_gather | solution.py:12
  34.7 93.8 %copy-start.5 = (bf16[2,768,384]{2,1,0:T(8,128)(2,1)S(1)}, bf16[2,768,384]{2,1,0:T(8,128)(2,1)}, u32[]{:S(2)}) copy-start(bf16[2,768,384]{2,1,0:T(8,128)(2,1)} %param.14) | copy-start | bytes 3538948
  34.7 203.7 %reduce-scatter.4.cloned.1.call-start = ((), (), s32[]{:S(2)}) async-start(), calls=%async_computation.8 | async-start | bytes 7077888 | tf_op jit(solution)/shard_map/reduce_scatter | solution.py:16
  122.6 6.0 copy-start.9
  128.6 5.7 copy-start.10
  134.3 1.8 copy-start.11
  141.3 0.7 copy-start.7
  141.3 3.7 copy-start.6
  141.3 4.1 copy-start.8
  141.3 120.9 %copy-start.2 = (bf16[128,768]{1,0:T(8,128)(2,1)S(1)}, bf16[128,768]{1,0:T(8,128)(2,1)}, u32[]{:S(2)}) copy-start(bf16[128,768]{1,0:T(8,128)(2,1)} %param.10) | copy-start | bytes 589828
  141.3 230.4 %all-gather.6.cloned.1.call-start = ((), (), s32[]{:S(2)}) async-start(), calls=%async_computation.9 | async-start | bytes 1585152 | tf_op jit(solution)/shard_map/all_gather | solution.py:88
  240.6 19.1 %all-to-all-start.1 = ((bf16[16,2,16,768]{3,2,1,0:T(8,128)(2,1)}), bf16[16,2,16,768]{3,2,1,0:T(8,128)(2,1)S(1)}, u32[]{:S(2)}, u32[]{:S(2)}) async-start(bf16[16,2,16,768]{3,2,1,0:T(8,128)(2,1)} %copy.84), calls=%async_computation.2 | async-start | bytes 1572864 | tf_op jit(solution)/shard_map/all_to_all | solution.py:19
  246.3 239.0 %all-gather.8.cloned.1.call-start = ((), (), s32[]{:S(2)}) async-start(), calls=%async_computation.11 | async-start | bytes 7077888 | tf_op jit(solution)/shard_map/all_gather | solution.py:12
  259.7 0.9 copy-start.4
  399.3 668.9 %reduce-scatter.6.cloned.1.call-start = ((), (), s32[]{:S(2)}) async-start(), calls=%async_computation.10 | async-start | bytes 3170304 | tf_op jit(solution)/shard_map/reduce_scatter | solution.py:93
  401.8 768.2 %reduce-scatter.8.cloned.1.call-start = ((), (), s32[]{:S(2)}) async-start(), calls=%async_computation.12 | async-start | bytes 7077888 | tf_op jit(solution)/shard_map/reduce_scatter | solution.py:16
  512.7 801.3 %all-reduce.2.cloned.1.call-start = ((), (), s32[]{:S(2)}) async-start(), calls=%async_computation.13 | async-start | bytes 196608 | tf_op jit(solution)/shard_map/psum | solution.py:130
  1172.2 22.3 %all-to-all-start.3 = ((bf16[16,2,16,768]{3,2,1,0:T(8,128)(2,1)}), bf16[16,2,16,768]{3,2,1,0:T(8,128)(2,1)S(1)}, u32[]{:S(2)}, u32[]{:S(2)}) async-start(bf16[16,2,16,768]{3,2,1,0:T(8,128)(2,1)} %copy.88), calls=%async_computation.6 | async-start | bytes 1572864 | tf_op jit(solution)/shard_map/all_to_all | solution.py:19
  1178.1 8.7 copy-start.3
  1186.8 128.8 %copy-start.1 = (bf16[2,384,768]{2,1,0:T(8,128)(2,1)S(1)}, bf16[2,384,768]{2,1,0:T(8,128)(2,1)}, u32[]{:S(2)}) copy-start(bf16[2,384,768]{2,1,0:T(8,128)(2,1)} %param.15) | copy-start | bytes 3538948
Sparse Core Ops, SparseCore 0:
  34.8 87.7 all-gather.3
  141.4 96.9 reduce-scatter.3
  399.4 85.8 all-gather.7
Sparse Core Ops, SparseCore 1:
  144.1 227.5 all-gather.5
  402.2 666.0 reduce-scatter.5
  1072.4 97.5 reduce-scatter.7
  1176.0 137.9 all-reduce.1
where the time goes:
time: 1320 us
  waiting for transfers between devices  1150 us (87%)
  matrix products  80.4 us (6%)
  blocking collectives  37.4 us (3%)
  local copies, waits for them, and re-layouts  17.9 us (1%)
  between operations  17.7 us (1%)
    reduce_scatter x1, waiting for transfers between devices, body(): lax.psum_scatter(jnp.einsum('st,sd->td', weights, embed_b, preferred_elem...  554 us
    reduce_scatter x2, waiting for transfers between devices, collect(): lax.psum_scatter(partial_out.astype(jnp.bfloat16), 'row', scatter_dimensi...  185 us
    all_gather x2, waiting for transfers between devices, spread(): return lax.all_gather(arrived, 'row', axis=0, tiled=True)  171 us
    psum x1, waiting for transfers between devices, body(): lax.psum(jnp.dot(norm_wide.T, score_grad, precision=lax.Precision.HIGHEST...  118 us
    all_gather x1, waiting for transfers between devices, body(): everyone = lax.all_gather(text_b, ('row', 'col'), axis=0, tiled=True)  109 us
    all_to_all x2, blocking collectives, spread(): lax.all_to_all(buffer, 'col', split_axis=0, concat_axis=0, tiled=True)  37.4 us
  transfers between devices with their start and end apart: 9, of which 8 were waited for; matrix products, arithmetic and copies ran while one was open for 5% of the time, Pallas kernels for 0%

commit v1 on v0

v1 whole, which is shorter than its diff:
```python
import functools
import types

import jax
import jax.numpy as jnp
from jax import lax
from jax.experimental import pallas as pl
from jax.experimental.pallas import tpu as pltpu
from jax.sharding import PartitionSpec as P

EXP_DEV = 2
SEQ = 16
F32 = jnp.float32
BF16 = jnp.bfloat16
MESH = pl.DeviceIdType.MESH
VMEM = pl.BlockSpec(memory_space=pltpu.VMEM)
SMEM = pl.BlockSpec(memory_space=pltpu.SMEM)
ANY = pl.BlockSpec(memory_space=pl.ANY)
N_ROW, N_COL, N_XZ = 8, 16, 8
GROUPS, PER_GROUP = 4, 4


def column_of(place):
    return (place % N_XZ) * 2 + place // N_XZ


def place_of(column):
    return (column % 2) * N_XZ + column // 2


def remote(src, dst, send_sem, recv_sem, row, col):
    return pltpu.make_async_remote_copy(
        src_ref=src, dst_ref=dst, send_sem=send_sem, recv_sem=recv_sem,
        device_id={"row": row, "col": col}, device_id_type=MESH,
    )


def here():
    row, col = lax.axis_index("row"), lax.axis_index("col")
    return row, col, col // 2, col % 2


def greet(all_columns, all_rows):
    row, col, xz, core = here()
    barrier = pltpu.get_barrier_semaphore()

    def signal(r, c):
        pl.semaphore_signal(barrier, inc=1, device_id={"row": r, "col": c}, device_id_type=MESH)

    count = 0
    if all_columns:
        def col_step(d, _):
            signal(row, (col + d) % N_COL)
            return 0
        lax.fori_loop(1, N_COL, col_step, 0)
        count += N_COL - 1
    else:
        def xz_step(d, _):
            signal(row, ((xz + d) % N_XZ) * 2 + core)
            return 0
        lax.fori_loop(1, N_XZ, xz_step, 0)
        signal(row, xz * 2 + 1 - core)
        count += N_XZ
    if all_rows:
        def row_step(d, _):
            signal((row + d) % N_ROW, col)
            return 0
        lax.fori_loop(1, N_ROW, row_step, 0)
        count += N_ROW - 1
    pl.semaphore_wait(barrier, count)


def loop(low, high, step):
    lax.fori_loop(low, high, lambda i, _: (step(i), 0)[1], 0)


class Gather:
    def __init__(self, stage, whole, sems):
        self.stage, self.whole = stage, whole
        self.s1, self.r1, self.s2, self.r2, self.s3, self.r3 = sems
        self.row, self.col, self.xz, self.core = here()

    def first(self, d):
        to = (self.row + d) % N_ROW
        mine = self.stage.at[self.row]
        return remote(mine, mine, self.s1.at[d - 1], self.r1.at[d - 1], to, self.col)

    def second(self, d):
        to = (self.xz + d) % N_XZ
        mine = self.whole.at[self.core, self.xz]
        return remote(mine, mine, self.s2.at[d - 1], self.r2.at[d - 1], self.row, to * 2 + self.core)

    def third(self):
        mine = self.whole.at[self.core]
        return remote(mine, mine, self.s3, self.r3, self.row, self.xz * 2 + 1 - self.core)

    def first_arrived(self, d):
        at = self.stage.at[(self.row + N_ROW - d) % N_ROW]
        remote(at, at, self.s1.at[d - 1], self.r1.at[d - 1], self.row, self.col).wait_recv()

    def second_arrived(self, d):
        at = self.whole.at[self.core, (self.xz + N_XZ - d) % N_XZ]
        remote(at, at, self.s2.at[d - 1], self.r2.at[d - 1], self.row, self.col).wait_recv()

    def start(self, rows):
        self.stage[self.row] = rows
        loop(1, N_ROW, lambda d: self.first(d).start())

    def spread(self):
        loop(1, N_ROW, self.first_arrived)
        block = self.stage[...]
        self.whole[self.core, self.xz] = block.reshape(-1, block.shape[-1]).astype(BF16)
        loop(1, N_XZ, lambda d: self.second(d).start())

    def swap(self):
        loop(1, N_XZ, self.second_arrived)
        self.third().start()

    def finish(self):
        at = self.whole.at[1 - self.core]
        remote(at, at, self.s3, self.r3, self.row, self.col).wait_recv()
        loop(1, N_ROW, lambda d: self.first(d).wait_send())
        loop(1, N_XZ, lambda d: self.second(d).wait_send())
        self.third().wait_send()


def gather_sems():
    dma = pltpu.SemaphoreType.DMA
    return [dma((N_ROW - 1,)), dma((N_ROW - 1,)), dma((N_XZ - 1,)), dma((N_XZ - 1,)), dma, dma]


def fused_kernel(names, *refs):
    n = types.SimpleNamespace(**dict(zip(names, refs)))
    row, col, xz, core = here()
    place = core * N_XZ + xz
    y, high = row % 4, row // 4
    other_row = (1 - high) * 4 + y
    width = n.tok_mean.shape[-1]
    units = n.w_gate.shape[-1]
    capacity = n.rows.shape[2]
    slots = N_COL * capacity
    records = N_COL * 8
    batch = N_ROW * records

    def row_of(rel, step):
        return ((high + rel) % 2) * 4 + (y + step + 4) % 4

    def arrived(at, sem):
        remote(at, at, n.a_send.at[0], sem, row, col).wait_recv()

    greet(True, True)

    def meta_part(d):
        to = (place + d) % N_COL
        return remote(n.meta.at[to], n.table.at[place], n.m_send.at[d - 1], n.m_recv.at[d - 1], row, column_of(to))

    def part(d):
        to = (place + d) % N_COL
        return remote(
            n.rows.at[to], n.grid.at[:, place, row], n.a_send.at[d - 1], n.a_recv.at[place], row, column_of(to)
        )

    loop(1, N_COL, lambda d: meta_part(d).start())
    own = pltpu.make_async_copy(n.rows.at[place], n.grid.at[:, place, row], n.own_sem)
    own.start()
    loop(1, N_COL, lambda d: part(d).start())
    texts = Gather(n.t_stage, n.everyone, [n.ts1, n.tr1, n.ts2, n.tr2, n.ts3, n.tr3])
    texts.start(n.text[...])
    n.table[place] = n.meta[place]
    loop(1, N_COL, lambda d: arrived(n.table.at[(place + N_COL - d) % N_COL], n.m_recv.at[d - 1]))
    n.compact[row] = jnp.sum(n.table[...].reshape(N_COL // 4, 4, 8, 128), 1)

    def table_copy(d):
        at = n.compact.at[row]
        return remote(at, at, n.c_send.at[d - 1], n.c_recv.at[d - 1], (row + d) % N_ROW, col)

    loop(1, N_ROW, lambda d: table_copy(d).start())

    def piece(ref, group, at_row):
        return ref.at[:, pl.ds(group * PER_GROUP, PER_GROUP), at_row]

    def across(group):
        at = piece(n.grid, group, row)
        return remote(at, at, n.x_send.at[group], n.x_recv.at[group], other_row, col)

    def near(way, rel, group):
        at = piece(n.grid, group, row_of(rel, 0))
        step = 1 - 2 * way
        return remote(at, at, n.n_send.at[way, rel, group], n.n_recv.at[way, rel, group], row_of(0, step), col)

    def far(way, rel, half):
        step = 1 - 2 * way
        at = piece(n.grid, 2 * way + half, row_of(rel, -step))
        return remote(at, at, n.f_send.at[way, rel, half], n.f_recv.at[way, rel, half], row_of(0, step), col)

    def iota(shape, dim):
        return lax.broadcasted_iota(jnp.int32, shape, dim)

    def forward(r):
        def one(x):
            tile = n.compact[r]
            spread = jnp.broadcast_to(tile[:, None], (4, 4, 8, 128)).reshape(records, 128)
            at = (records, 128)
            spread = jnp.where(iota(at, 1) // 32 == (iota(at, 0) // 8) % 4, spread, 0.0).astype(BF16)
            at = (128, slots)
            pick = (iota(at, 0) % 32 == x * capacity + iota(at, 1) % capacity).astype(F32).astype(BF16)
            at = (records, slots)
            pool = jnp.dot(spread, pick, preferred_element_type=F32)
            pool = jnp.where(iota(at, 0) // 8 == iota(at, 1) // capacity, pool, 0.0).astype(BF16)
            at = (slots, 128)
            pick = (iota(at, 1) % 32 == x * capacity + iota(at, 0) % capacity).astype(F32).astype(BF16)
            at = (slots, records)
            turned = lax.dot_general(pick, spread, (((1,), (1,)), ((), ())), preferred_element_type=F32)
            n.turned[r, x] = jnp.where(iota(at, 1) // 8 == iota(at, 0) // capacity, turned, 0.0).astype(BF16)
            rows = n.grid[x, :, r].reshape(slots, width)
            gate_pre = jnp.dot(rows, n.w_gate[x], preferred_element_type=F32)
            up_pre = jnp.dot(rows, n.w_up[x], preferred_element_type=F32)
            sigma = jax.nn.sigmoid(gate_pre)
            silu_gate = gate_pre * sigma
            hidden = (silu_gate * up_pre).astype(BF16)
            shape = (N_COL, capacity, units)
            n.hidden[x, :, r] = hidden.reshape(shape)
            n.for_gate[x, :, r] = (up_pre * (sigma * (1.0 + gate_pre * (1.0 - sigma)))).astype(BF16).reshape(shape)
            n.for_up[x, :, r] = silu_gate.astype(BF16).reshape(shape)
            n.acc[x, :, r] = jnp.dot(pool, hidden, preferred_element_type=F32).reshape(N_COL, 8, units)
        loop(0, EXP_DEV, one)

    own.wait()
    for group in range(GROUPS):
        def one(i, group=group):
            from_place = group * PER_GROUP + i

            @pl.when(from_place != place)
            def _():
                arrived(n.grid.at[:, from_place, row], n.a_recv.at[from_place])
        loop(0, PER_GROUP, one)
        across(group).start()
        near(0, 0, group).start()
        near(1, 0, group).start()

    def neighbour(way, rel, group):
        step = 1 - 2 * way
        arrived(piece(n.grid, group, row_of(rel, -step)), n.n_recv.at[way, rel, group])
        if group // 2 == way:
            far(way, rel, group % 2).start()

    texts.spread()
    forward(row)
    loop(1, N_ROW, lambda d: arrived(n.compact.at[(row + N_ROW - d) % N_ROW], n.c_recv.at[d - 1]))
    for group in range(GROUPS):
        arrived(piece(n.grid, group, other_row), n.x_recv.at[group])
        near(0, 1, group).start()
        near(1, 1, group).start()
        neighbour(0, 0, group)
        neighbour(1, 0, group)
    texts.swap()
    forward(other_row)
    loop(0, 2, lambda way: forward(row_of(0, 2 * way - 1)))
    for group in range(GROUPS):
        neighbour(0, 1, group)
        neighbour(1, 1, group)
    loop(0, 2, lambda way: forward(row_of(1, 2 * way - 1)))
    for rel in range(2):
        for half in range(2):
            for way in range(2):
                arrived(piece(n.grid, 2 * way + half, row_of(rel, 2)), n.f_recv.at[way, rel, half])
        forward(row_of(rel, 2))

    def quarter(q):
        return n.hb[0, q], n.hb[1, q]

    def round_pooled(q):
        for x in range(EXP_DEV):
            n.hb[x, q] = n.acc[x, pl.ds(q * 4, 4)].reshape(-1, units).astype(BF16)

    def share(q):
        first, second = quarter(q)
        total = jnp.dot(first, n.w_down[0], preferred_element_type=F32) + jnp.dot(
            second, n.w_down[1], preferred_element_type=F32
        )
        n.part[q // 2, pl.ds((q % 2) * 4, 4)] = total.astype(BF16).reshape(4, -1, width)

    loop(0, 4, round_pooled)
    loop(0, 2, lambda i: share((1 - core) * 2 + i))
    swap = remote(n.part.at[1 - core], n.half, n.s1, n.r1, row, xz * 2 + 1 - core)
    swap.start()
    loop(0, 2, lambda i: share(core * 2 + i))
    swap.wait()

    def add(i):
        n.sums[i] = (n.part[core, i].astype(F32) + n.half[i].astype(F32)).astype(BF16)

    loop(0, N_XZ, add)

    def to_chip(d):
        to = (xz + d) % N_XZ
        return remote(n.sums.at[to], n.from_xz.at[d - 1], n.s2.at[d - 1], n.r2.at[d - 1], row, to * 2 + core)

    loop(1, N_XZ, lambda d: to_chip(d).start())
    loop(1, N_XZ, lambda d: to_chip(d).wait_recv())
    total = n.sums[xz].astype(F32)
    for d in range(N_XZ - 1):
        total = total + n.from_xz[d].astype(F32)
    n.sums_row[...] = total.reshape(n.sums_row.shape)

    def to_row(d):
        to = (row + d) % N_ROW
        return remote(n.sums_row.at[to], n.from_row.at[d - 1], n.s3.at[d - 1], n.r3.at[d - 1], to, col)

    loop(1, N_ROW, lambda d: to_row(d).start())
    texts.finish()
    loop(1, N_ROW, lambda d: to_row(d).wait_recv())
    total = n.sums_row[row]
    for d in range(N_ROW - 1):
        total = total + n.from_row[d]
    pooled = n.tok_mean[...] + total * (1.0 / SEQ)
    pooled_norm = jnp.sqrt(jnp.sum(pooled * pooled, -1, keepdims=True) + 1e-06)
    embed = pooled / pooled_norm
    embed_b = embed.astype(BF16)
    embeds = Gather(n.e_stage, n.e_whole, [n.es1, n.er1, n.es2, n.er2, n.es3, n.er3])
    grads = Gather(n.g_stage, n.grads, [n.gs1, n.gr1, n.gs2, n.gr2, n.gs3, n.gr3])
    embeds.start(embed_b.astype(F32))
    scale, shift, factor = n.scalars[0], n.scalars[1], n.scalars[2]
    at = (8, batch)
    same = (place * N_ROW + row) * 8 + iota(at, 0) == iota(at, 1)
    labels = jnp.where(same, 1.0, -1.0).astype(F32)

    def weigh(mine, others):
        logits = scale * lax.dot_general(mine, others, (((1,), (1,)), ((), ())), preferred_element_type=F32) + shift
        weights = (-factor * labels * jax.nn.sigmoid(-labels * logits)).astype(BF16)
        return jnp.dot(weights, others, preferred_element_type=F32)

    embed_grad = weigh(embed_b, n.everyone[...].reshape(batch, width))
    pooled_grad = (embed_grad - embed * jnp.sum(embed * embed_grad, -1, keepdims=True)) / pooled_norm
    out_grad = pooled_grad * (1.0 / SEQ)
    n.own_grad[...] = out_grad
    grads.start(out_grad)
    grads.spread()
    grads.swap()
    grads.finish()

    def through_down(q):
        block = n.grads[q // 2, pl.ds((q % 2) * 4, 4)].reshape(-1, width)
        for x in range(EXP_DEV):
            back = lax.dot_general(block, n.w_down[x], (((1,), (1,)), ((), ())), preferred_element_type=F32)
            n.acc[x, pl.ds(q * 4, 4)] = back.reshape(4, N_ROW, 8, units)

    def backward(r):
        n.q[r] = jnp.zeros(n.q.shape[1:], F32)

        def one(x):
            back = n.acc[x, :, r].reshape(records, units).astype(BF16)
            hidden_grad = jnp.dot(n.turned[r, x], back, preferred_element_type=F32)
            shape = (N_COL, capacity, units)
            hidden = n.hidden[x, :, r].reshape(slots, units).astype(F32)
            q = jnp.sum(hidden * hidden_grad, -1, keepdims=True)
            at = (slots, 128)
            q = jnp.where(iota(at, 1) == x * capacity + iota(at, 0) % capacity, q, 0.0)
            n.q[r] += jnp.sum(q.reshape(N_COL, capacity, 128), 1)
            gate_delta = (hidden_grad * n.for_gate[x, :, r].reshape(slots, units).astype(F32)).astype(BF16)
            up_delta = (hidden_grad * n.for_up[x, :, r].reshape(slots, units).astype(F32)).astype(BF16)
            n.for_gate[x, :, r] = gate_delta.reshape(shape)
            n.for_up[x, :, r] = up_delta.reshape(shape)
            dims = (((1,), (1,)), ((), ()))
            total = lax.dot_general(gate_delta, n.w_gate[x], dims, preferred_element_type=F32)
            total = total + lax.dot_general(up_delta, n.w_up[x], dims, preferred_element_type=F32)
            n.back[x, :, r] = total.astype(BF16).reshape(N_COL, capacity, width)
        loop(0, EXP_DEV, one)

    def far_back(way, rel, half):
        return remote(
            piece(n.back, 2 * way + half, row_of(rel, 2)), n.far_buf.at[way, rel, half],
            n.bf_send.at[way, rel, half], n.bf_recv.at[way, rel, half], row_of(0, 1 - 2 * way), col,
        )

    def near_back(way, rel, group):
        step = 1 - 2 * way
        mine = group // 2 == way
        src = n.far_buf.at[way, rel, group % 2] if mine else piece(n.back, group, row_of(rel, step))
        return remote(
            src, n.near_buf.at[way, rel, group],
            n.bn_send.at[way, rel, group], n.bn_recv.at[way, rel, group], row_of(0, step), col,
        )

    def across_back(group):
        return remote(
            n.near_buf.at[0, 1, group], n.x_buf.at[group], n.bx_send.at[group], n.bx_recv.at[group], other_row, col
        )

    def add_into(target, *terms):
        def one(k):
            x, i = k // PER_GROUP, k % PER_GROUP
            total = terms[0][x, i].astype(F32)
            for term in terms[1:]:
                total = total + term[x, i].astype(F32)
            target[x, i] = total.astype(BF16)
        loop(0, EXP_DEV * PER_GROUP, one)

    def q_row(d):
        to = (row + d) % N_ROW
        return remote(n.q.at[to], n.q_buf.at[d - 1], n.q1_send.at[d - 1], n.q1_recv.at[d - 1], to, col)

    loop(0, 4, through_down)
    for rel in (1, 0):
        backward(row_of(rel, 2))
        for half in range(2):
            for way in range(2):
                far_back(way, rel, half).start()
    for rel in (1, 0):
        loop(0, 2, lambda way, rel=rel: backward(row_of(rel, 1 - 2 * way)))
        for half in range(2):
            for way in range(2):
                near_back(way, rel, 2 * (1 - way) + half).start()
    backward(other_row)
    backward(row)
    loop(1, N_ROW, lambda d: q_row(d).start())
    embeds.spread()
    for rel in (1, 0):
        for half in range(2):
            for way in range(2):
                far_back(way, rel, half).wait_recv()
                at = n.far_buf.at[way, rel, half]
                add_into(at, at, piece(n.back, 2 * way + half, row_of(rel, 1 - 2 * way)))
                near_back(way, rel, 2 * way + half).start()
    loop(1, N_ROW, lambda d: q_row(d).wait_recv())
    total = n.q[row]
    for d in range(N_ROW - 1):
        total = total + n.q_buf[d]
    n.q_msg[...] = jnp.broadcast_to(total[:, None, :], n.q_msg.shape)
    n.q_in[place] = n.q_msg[place]

    def q_col(d):
        to = (place + d) % N_COL
        return remote(n.q_msg.at[to], n.q_in.at[place], n.q2_send.at[d - 1], n.q2_recv.at[d - 1], row, column_of(to))

    loop(1, N_COL, lambda d: q_col(d).start())
    embeds.swap()

    def weight_grads(x):
        dims = (((0,), (0,)), ((), ()))

        def one(t):
            at = pl.ds(pl.multiple_of(t * 256, 256), 256)
            rows = n.grid[x, :, :, :, at].reshape(-1, 256)
            n.gate_out[x, at] = lax.dot_general(
                rows, n.for_gate[x].reshape(-1, units), dims, preferred_element_type=F32
            )
            n.up_out[x, at] = lax.dot_general(
                rows, n.for_up[x].reshape(-1, units), dims, preferred_element_type=F32
            )
        loop(0, width // 256, one)
        pltpu.make_async_copy(n.gate_out.at[x], n.d_gate.at[x], n.out_sem.at[0, x]).start()
        pltpu.make_async_copy(n.up_out.at[x], n.d_up.at[x], n.out_sem.at[1, x]).start()

    weight_grads(0)
    loop(1, N_COL, lambda d: arrived(n.q_in.at[(place + N_COL - d) % N_COL], n.q2_recv.at[d - 1]))
    ids = n.ids[...]
    gates = n.gates[...]
    found = []
    for k in range(2):
        at = (ids.shape[0], N_COL)
        by_place = (iota(at, 1) == ids[:, k : k + 1]).astype(F32)
        lines = jnp.dot(by_place, n.q_in[:, 0, :], precision=lax.Precision.HIGHEST, preferred_element_type=F32)
        at = (ids.shape[0], 128)
        found.append(jnp.sum(jnp.where(iota(at, 1) == ids[:, 2 + k : 3 + k], lines, 0.0), -1, keepdims=True))
    both = found[0] + found[1]
    score_grad = jnp.zeros((ids.shape[0], 128), F32)
    for k in range(2):
        logit_grad = found[k] - gates[:, k : k + 1] * both
        score_grad = score_grad + jnp.where(iota(score_grad.shape, 1) == ids[:, 4 + k : 5 + k], logit_grad, 0.0)
    n.score_grad[...] = score_grad
    router_part = jnp.dot(
        score_grad.T[: EXP_DEV * N_COL], n.norm[...], precision=lax.Precision.HIGHEST, preferred_element_type=F32
    )
    for i in range(4):
        for j in range(2):
            n.dr[j * 4 + i] = router_part[i * 8 : i * 8 + 8, j * (width // 2) : (j + 1) * (width // 2)]

    def scatter(d):
        to = (row + d) % N_ROW
        return remote(n.dr.at[to], n.dr_in.at[row], n.d1_send.at[d - 1], n.d1_recv.at[d - 1], to, col)

    def tell_col(d):
        at = n.dr_sum.at[col]
        return remote(at, at, n.d2_send.at[d - 1], n.d2_recv.at[d - 1], row, (col + d) % N_COL)

    def tell_row(d):
        at = n.d_router.at[row]
        return remote(at, at, n.d3_send.at[d - 1], n.d3_recv.at[d - 1], (row + d) % N_ROW, col)

    loop(1, N_ROW, lambda d: scatter(d).start())
    n.dr_in[row] = n.dr[row]
    for group in (2, 0, 3, 1):
        for way in range(2):
            near_back(way, 1, group).wait_recv()
        at = n.near_buf.at[0, 1, group]
        add_into(at, at, n.near_buf.at[1, 1, group], piece(n.back, group, other_row))
        across_back(group).start()
    loop(1, N_ROW, lambda d: arrived(n.dr_in.at[(row + N_ROW - d) % N_ROW], n.d1_recv.at[d - 1]))
    n.dr_sum[col] = jnp.sum(n.dr_in[...], 0)
    loop(1, N_COL, lambda d: tell_col(d).start())
    weight_grads(1)

    def down_grads(x):
        def one(t):
            at = pl.ds(pl.multiple_of(t * 128, 128), 128)
            n.down_out[x, at] = lax.dot_general(
                n.hb[x, :, :, at].reshape(-1, 128), n.grads[...].reshape(batch, width),
                (((0,), (0,)), ((), ())), preferred_element_type=F32,
            )
        loop(0, units // 128, one)
        pltpu.make_async_copy(n.down_out.at[x], n.d_down.at[x], n.out_sem.at[2, x]).start()

    down_grads(0)
    down_grads(1)
    loop(1, N_COL, lambda d: arrived(n.dr_sum.at[(col + N_COL - d) % N_COL], n.d2_recv.at[d - 1]))
    n.d_router[row] = jnp.sum(n.dr_sum[...], 0)
    loop(1, N_ROW, lambda d: tell_row(d).start())
    embeds.finish()
    text_unit = n.text[...]
    text_grad = weigh(text_unit.astype(BF16), n.e_whole[...].reshape(batch, width))
    n.d_text[...] = (text_grad - text_unit * jnp.sum(text_unit * text_grad, -1, keepdims=True)) / n.text_norm[...]

    def home(group, i):
        to = group * PER_GROUP + i
        return remote(
            n.sum_buf.at[group, :, i], n.slots.at[place], n.h_send.at[to], n.h_recv.at[place], row, column_of(to)
        )

    def own_home(group, i):
        return pltpu.make_async_copy(n.sum_buf.at[group, :, i], n.slots.at[place], n.own_sem)

    for group in (2, 0, 3, 1):
        for way in range(2):
            near_back(way, 0, group).wait_recv()
        across_back(group).wait_recv()
        add_into(
            n.sum_buf.at[group], n.near_buf.at[0, 0, group], n.near_buf.at[1, 0, group], n.x_buf.at[group],
            piece(n.back, group, row),
        )

        def send(i, group=group):
            @pl.when(group * PER_GROUP + i != place)
            def _():
                home(group, i).start()

            @pl.when(group * PER_GROUP + i == place)
            def _():
                own_home(group, i).start()
        loop(0, PER_GROUP, send)

    loop(1, N_ROW, lambda d: arrived(n.d_router.at[(row + N_ROW - d) % N_ROW], n.d3_recv.at[d - 1]))
    loop(1, N_COL, lambda d: meta_part(d).wait_send())
    loop(1, N_COL, lambda d: part(d).wait_send())
    loop(1, N_COL, lambda d: q_col(d).wait_send())
    loop(1, N_COL, lambda d: tell_col(d).wait_send())
    loop(1, N_ROW, lambda d: table_copy(d).wait_send())
    loop(1, N_ROW, lambda d: to_row(d).wait_send())
    loop(1, N_ROW, lambda d: q_row(d).wait_send())
    loop(1, N_ROW, lambda d: scatter(d).wait_send())
    loop(1, N_ROW, lambda d: tell_row(d).wait_send())
    loop(1, N_XZ, lambda d: to_chip(d).wait_send())
    for group in range(GROUPS):
        across(group).wait_send()
        across_back(group).wait_send()
        for way in range(2):
            for rel in range(2):
                near(way, rel, group).wait_send()
                near_back(way, rel, group).wait_send()
    for rel in range(2):
        for half in range(2):
            for way in range(2):
                far(way, rel, half).wait_send()
                far_back(way, rel, half).wait_send()
    for x in range(EXP_DEV):
        pltpu.make_async_copy(n.gate_out.at[x], n.d_gate.at[x], n.out_sem.at[0, x]).wait()
        pltpu.make_async_copy(n.up_out.at[x], n.d_up.at[x], n.out_sem.at[1, x]).wait()
        pltpu.make_async_copy(n.down_out.at[x], n.d_down.at[x], n.out_sem.at[2, x]).wait()
    loop(1, N_COL, lambda d: arrived(n.slots.at[(place + N_COL - d) % N_COL], n.h_recv.at[(place + N_COL - d) % N_COL]))
    own_home(0, 0).wait()
    for group in range(GROUPS):
        def sent(i, group=group):
            @pl.when(group * PER_GROUP + i != place)
            def _():
                home(group, i).wait_send()
        loop(0, PER_GROUP, sent)


def fused(ins):
    width = ins["tok_mean"].shape[-1]
    units = ins["w_gate"].shape[-1]
    tok_count = ins["ids"].shape[0]
    capacity = ins["rows"].shape[2]
    slots, records = N_COL * capacity, N_COL * 8
    whole = (2, N_XZ, N_ROW * 8, width)
    block = (EXP_DEV, PER_GROUP, capacity, width)
    grid = (EXP_DEV, N_COL, N_ROW, capacity)
    outs = {
        "own_grad": ((8, width), F32, VMEM),
        "d_text": ((8, width), F32, VMEM),
        "slots": ((N_COL, EXP_DEV, capacity, width), BF16, VMEM),
        "score_grad": ((tok_count, 128), F32, VMEM),
        "d_router": ((N_ROW, 8, width // 2), F32, VMEM),
        "d_gate": (ins["w_gate"].shape, F32, ANY),
        "d_up": (ins["w_up"].shape, F32, ANY),
        "d_down": (ins["w_down"].shape, F32, ANY),
    }
    scratch = {
        "grid": (grid + (width,), BF16),
        "table": ((N_COL, 8, 128), F32),
        "compact": ((N_ROW, N_COL // 4, 8, 128), F32),
        "t_stage": ((N_ROW, 8, width), F32),
        "everyone": (whole, BF16),
        "turned": ((N_ROW, EXP_DEV, slots, records), BF16),
        "hidden": (grid + (units,), BF16),
        "for_gate": (grid + (units,), BF16),
        "for_up": (grid + (units,), BF16),
        "acc": ((EXP_DEV, N_COL, N_ROW, 8, units), F32),
        "hb": ((EXP_DEV, 4, N_ROW * records // 4, units), BF16),
        "part": (whole, BF16),
        "half": (whole[1:], BF16),
        "sums": (whole[1:], BF16),
        "from_xz": ((N_XZ - 1,) + whole[2:], BF16),
        "sums_row": ((N_ROW, 8, width), F32),
        "from_row": ((N_ROW - 1, 8, width), F32),
        "e_stage": ((N_ROW, 8, width), F32),
        "e_whole": (whole, BF16),
        "g_stage": ((N_ROW, 8, width), F32),
        "grads": (whole, BF16),
        "back": (grid + (width,), BF16),
        "far_buf": ((2, 2, 2) + block, BF16),
        "near_buf": ((2, 2, GROUPS) + block, BF16),
        "x_buf": ((GROUPS,) + block, BF16),
        "sum_buf": ((GROUPS,) + block, BF16),
        "q": ((N_ROW, N_COL, 128), F32),
        "q_buf": ((N_ROW - 1, N_COL, 128), F32),
        "q_msg": ((N_COL, 8, 128), F32),
        "q_in": ((N_COL, 8, 128), F32),
        "dr": ((N_ROW, 8, width // 2), F32),
        "dr_in": ((N_ROW, 8, width // 2), F32),
        "dr_sum": ((N_COL, 8, width // 2), F32),
        "gate_out": (ins["w_gate"].shape, F32),
        "up_out": (ins["w_up"].shape, F32),
        "down_out": (ins["w_down"].shape, F32),
    }
    row, col, chips = (N_ROW - 1,), (N_COL - 1,), (N_XZ - 1,)
    sems = {
        "own_sem": (), "out_sem": (3, EXP_DEV),
        "m_send": col, "m_recv": col, "a_send": col, "a_recv": (N_COL,), "c_send": row, "c_recv": row,
        "x_send": (GROUPS,), "x_recv": (GROUPS,), "n_send": (2, 2, GROUPS), "n_recv": (2, 2, GROUPS),
        "f_send": (2, 2, 2), "f_recv": (2, 2, 2),
        "s1": (), "r1": (), "s2": chips, "r2": chips, "s3": row, "r3": row,
        "bf_send": (2, 2, 2), "bf_recv": (2, 2, 2), "bn_send": (2, 2, GROUPS), "bn_recv": (2, 2, GROUPS),
        "bx_send": (GROUPS,), "bx_recv": (GROUPS,), "h_send": (N_COL,), "h_recv": (N_COL,),
        "q1_send": row, "q1_recv": row, "q2_send": col, "q2_recv": col,
        "d1_send": row, "d1_recv": row, "d2_send": col, "d2_recv": col, "d3_send": row, "d3_recv": row,
    }
    for letter in "teg":
        for kind in "sr":
            sems.update({letter + kind + "1": row, letter + kind + "2": chips, letter + kind + "3": ()})
    names = list(ins) + list(outs) + list(scratch) + list(sems)
    result = pl.pallas_call(
        functools.partial(fused_kernel, names),
        out_shape=tuple(jax.ShapeDtypeStruct(shape, dtype) for shape, dtype, _ in outs.values()),
        in_specs=[SMEM if name == "scalars" else VMEM for name in ins],
        out_specs=tuple(spec for _, _, spec in outs.values()),
        scratch_shapes=[pltpu.VMEM(shape, dtype) for shape, dtype in scratch.values()]
        + [pltpu.SemaphoreType.DMA(shape) for shape in sems.values()],
        compiler_params=pltpu.CompilerParams(
            collective_id=0, has_side_effects=True, vmem_limit_bytes=61 << 20
        ),
    )(*ins.values())
    return dict(zip(outs, result))


def body(tokens, expert_ids, text, w_gate, w_up, w_down, router, log_scale, bias, loss_scale):
    tok_count, width = tokens.shape
    samples = tok_count // SEQ
    experts = EXP_DEV * N_COL
    capacity = max(2, 4 * tok_count // experts)
    line = EXP_DEV * capacity
    batch = samples * N_ROW * N_COL
    token_wide = tokens.astype(F32)
    inverse_rms = lax.rsqrt(jnp.mean(token_wide * token_wide, -1, keepdims=True) + 1e-06)
    normed = token_wide * inverse_rms
    norm_in = normed.astype(BF16)
    norm_wide = norm_in.astype(F32)
    scores = jnp.dot(norm_wide, router, precision=lax.Precision.HIGHEST)
    choose = (expert_ids[:, :, None] == jnp.arange(experts, dtype=jnp.int32)[None, None, :]).astype(F32)
    chosen = jnp.sum(choose * scores[:, None, :], -1)
    gates = jax.nn.sigmoid(chosen - chosen[:, ::-1])
    member = jnp.sum(choose, 1)
    before = jnp.cumsum(member, 0) - member
    position = jnp.sum(choose * before[:, None, :], -1).astype(jnp.int32)
    to_place = place_of(expert_ids // EXP_DEV)
    in_line = (expert_ids % EXP_DEV) * capacity + position
    slot_index = to_place * line + in_line
    slot = jnp.arange(experts * capacity, dtype=jnp.int32)[:, None]
    hit0 = slot_index[:, 0][None, :] == slot
    hit1 = slot_index[:, 1][None, :] == slot
    both = (hit0 | hit1).astype(BF16)
    outgoing = jnp.dot(both, norm_in, preferred_element_type=F32).astype(BF16)
    slot_gate = jnp.sum(
        jnp.where(hit0, gates[:, 0][None, :], 0.0) + jnp.where(hit1, gates[:, 1][None, :], 0.0), -1
    )
    record = (jnp.arange(tok_count, dtype=jnp.int32) // SEQ)[None, :]
    slot_record = jnp.sum(jnp.where(hit0 | hit1, record, 0), -1)
    in_record = slot_record.reshape(N_COL, 1, line) == jnp.arange(samples, dtype=jnp.int32)[None, :, None]
    meta = jnp.where(in_record, slot_gate.reshape(N_COL, 1, line), 0.0)
    own_place = place_of(lax.axis_index("col"))
    mine = (jnp.arange(128, dtype=jnp.int32) // line == own_place % 4)[None, None, :]
    meta = jnp.where(mine, jnp.tile(meta, (1, 1, 128 // line)), 0.0)
    text_wide = text.astype(F32)
    text_norm = jnp.sqrt(jnp.sum(text_wide * text_wide, -1, keepdims=True) + 1e-06)
    scale = jnp.exp(log_scale[0])
    got = fused({
        "scalars": jnp.stack([scale, bias[0], loss_scale[0] * scale / batch]),
        "rows": outgoing.reshape(N_COL, EXP_DEV, capacity, width),
        "meta": meta,
        "text": text_wide / text_norm,
        "text_norm": text_norm,
        "tok_mean": jnp.mean(token_wide.reshape(samples, SEQ, width), 1),
        "w_gate": w_gate,
        "w_up": w_up,
        "w_down": w_down,
        "ids": jnp.concatenate([to_place, in_line, expert_ids, expert_ids], -1),
        "gates": gates,
        "norm": norm_wide,
    })
    input_sum = lax.dot_general(
        both, got["slots"].reshape(-1, width), (((0,), (0,)), ((), ())), preferred_element_type=F32
    )
    score_grad = got["score_grad"][:, :experts]
    out_grad = jnp.repeat(got["own_grad"], SEQ, axis=0)
    norm_grad = input_sum + jnp.dot(score_grad, router.T, precision=lax.Precision.HIGHEST)
    d_tokens = out_grad + inverse_rms * (norm_grad - normed * jnp.mean(norm_grad * normed, -1, keepdims=True))
    d_router = got["d_router"].reshape(2, experts, width // 2).transpose(0, 2, 1).reshape(width, experts)
    return (got["d_text"], d_tokens, got["d_gate"], got["d_up"], got["d_down"], d_router)


def solution(mesh):
    in_specs = (
        P(("row", "col"), None),
        P(("row", "col"), None),
        P(("row", "col"), None),
        P("col", None, "row"),
        P("col", None, "row"),
        P("col", "row", None),
        P(),
        P(),
        P(),
        P(),
    )
    out_specs = (
        P(("row", "col"), None),
        P(("row", "col"), None),
        P("col", None, "row"),
        P("col", None, "row"),
        P("col", "row", None),
        P(),
    )
    return jax.shard_map(body, mesh=mesh, in_specs=in_specs, out_specs=out_specs, check_vma=False)
```

time: 1320 us -> 233 us (0.18)
  waiting for transfers between devices: 1150 us -> 0 us
  Pallas kernels: 0 us -> 202 us
  matrix products: 80.4 us -> 5.44 us
  blocking collectives: 37.4 us -> 0 us
  between operations: 17.7 us -> 2.88 us
    reduce_scatter x3 -> x0, waiting for transfers between devices: 739 us -> none  [the longest x1 554 us: body(): lax.psum_scatter(jnp.einsum('st,sd->td', weights, embed_b, preferred_elem...]
    all_gather x3 -> x0, waiting for transfers between devices: 280 us -> none  [the longest x2 171 us: spread(): return lax.all_gather(arrived, 'row', axis=0, tiled=True)]
    pallas_call x0 -> x1, Pallas kernels: none -> 202 us  [fused(): pl.pallas_call(functools.partial(fused_kernel, names), out_shape=tuple((j...]
    psum x1 -> x0, waiting for transfers between devices: 118 us -> none  [body(): lax.psum(jnp.dot(norm_wide.T, score_grad, precision=lax.Precision.HIGHEST...]
    dot_general x17 -> x2, matrix products: 79.4 us -> 2.77 us  [the longest x1 1.45 us: body(): lax.dot_general(both, got['slots'].reshape(-1, width), (((0,), (0,)), (()...]
    all_to_all x2 -> x0, blocking collectives: 37.4 us -> none  [spread(): lax.all_to_all(buffer, 'col', split_axis=0, concat_axis=0, tiled=True)]
  transfers between devices with their start and end apart: 9 -> 0, of which waited for: 8 -> 0; matrix products, arithmetic and copies ran while one was open for 5% -> 0% of each run, Pallas kernels for 0% -> 0%
where the time goes in v1:
time: 233 us; the launch traced here: 232 us
  Pallas kernels  202 us (87%)
  local copies, waits for them, and re-layouts  11.1 us (5%)
  other arithmetic  10.7 us (5%)
  matrix products  5.44 us (2%)
  between operations  2.88 us (1%)
    pallas_call x1, Pallas kernels, fused(): pl.pallas_call(functools.partial(fused_kernel, names), out_shape=tuple((j...  202 us
    unnamed x20, local copies, waits for them, and re-layouts  7.08 us

profile of v1, /device:TPU:1, one launch (start us, length us, event | category | flops | bytes accessed | tf_op | source)
XLA Modules:
  0.0 232.1 jit_solution(6743034984206934610)
XLA Ops:
  0.6 0.0 copy-start
  0.6 0.0 copy-start.1
  2.7 0.6 pad_maximum_fusion.refs_0_
  3.3 0.8 fusion.10
  4.2 1.0 multiply_reduce_fusion.1
  5.2 0.7 copy.62.refs_4_
  5.9 0.0 copy-done
  5.9 1.3 fusion.18
  7.2 0.7 convert_reduce_fusion
  7.9 1.0 bitcast_reduce_fusion
  8.9 1.4 convert_divide_fusion
  10.3 0.1 copy.55
  10.4 0.2 reduce_window_sum.11
  10.6 0.1 copy.57
  10.7 0.7 select_reduce_fusion.1
  11.4 0.7 multiply_add_fusion
  12.1 0.1 select_reduce_fusion
  12.2 0.8 pad_add_fusion
  13.0 0.1 eq.91
  13.1 0.7 copy.63.refs_9_
  13.8 0.1 copy.59
  13.9 0.1 rev.3
  14.0 0.0 copy-start.5
  14.1 0.2 slice_reduce_fusion.1
  14.2 0.2 add_reduce_fusion
  14.4 0.1 broadcast_in_dim.82
  14.5 0.1 tile.4
  14.6 0.2 tile.10
  14.7 0.6 broadcast_select_fusion.refs_2_
  15.4 0.0 copy-done.1
  15.4 0.8 fusion.17.refs_11_
  16.2 1.3 convolution_convert_fusion
  17.5 0.0 copy-done.5
  17.5 202.0 %shard_map.145 = (f32[8,768]{1,0:T(8,128)}, f32[8,768]{1,0:T(8,128)}, bf16[16,2,16,768]{3,2,1,0:T(8,128)(2,1)}, f32[128,128]{1,0:T(8,128)}, f32[8,8,384]{2,1,0:T...) custom-call(f32[3]{0:T(128)} %pad_maximum_fusion.refs_0_, ...), custom_call_target="tpu_custom_call" | custom-call | tf_op jit(solution)/shard_map/pallas_call | solution.py:662
  219.5 0.0 copy-start.7
  219.5 0.0 copy-start.6
  219.5 0.0 copy-start.4
  219.5 1.7 copy.65
  221.2 1.4 fusion.1
  222.7 1.4 multiply_reduce_fusion
  224.1 0.0 copy-done.7
  224.1 0.9 bitcast_add_fusion
  225.0 0.0 copy-done.6
  225.0 0.6 copy.73
  225.7 0.0 copy-done.4
  225.7 0.0 copy-start.3
  225.7 1.4 copy.74
  227.1 1.1 copy-done.3
  228.2 0.0 copy-start.2
  228.2 1.4 copy.75
  229.6 1.1 copy-done.2
  230.7 1.4 copy.76
  (9 shorter events, 0.1 us)
Async XLA Ops:
  0.6 5.3 %copy-start = (f32[768,32]{0,1:T(8,128)S(1)}, f32[768,32]{0,1:T(8,128)}, u32[]{:S(2)}) copy-start(f32[768,32]{0,1:T(8,128)} %param.16) | copy-start | bytes 294916
  0.6 14.7 %copy-start.1 = (bf16[128,768]{1,0:T(8,128)(2,1)S(1)}, bf16[128,768]{1,0:T(8,128)(2,1)}, u32[]{:S(2)}) copy-start(bf16[128,768]{1,0:T(8,128)(2,1)} %param.10) | copy-start | bytes 589828
  14.0 3.5 %copy-start.5 = (f32[128,2]{1,0:T(8,128)}, f32[128,2]{1,0:T(8,128)S(1)}, u32[]{:S(2)}) copy-start(f32[128,2]{1,0:T(8,128)S(1)} %add_divide_fusion.refs_10_) | copy-start | bytes 3076
  219.5 4.6 %copy-start.7 = (f32[8,768]{1,0:T(8,128)S(1)}, f32[8,768]{1,0:T(8,128)}, u32[]{:S(2)}) copy-start(f32[8,768]{1,0:T(8,128)} %get-tuple-element.15) | copy-start | bytes 73732
  219.5 5.5 %copy-start.6 = (f32[8,768]{1,0:T(8,128)S(1)}, f32[8,768]{1,0:T(8,128)}, u32[]{:S(2)}) copy-start(f32[8,768]{1,0:T(8,128)} %get-tuple-element.43) | copy-start | bytes 73732
  219.5 6.1 %copy-start.4 = (f32[2,768,384]{2,1,0:T(8,128)S(1)}, f32[2,768,384]{2,1,0:T(8,128)}, u32[]{:S(2)}) copy-start(f32[2,768,384]{2,1,0:T(8,128)} %get-tuple-element.45) | copy-start | bytes 7077892
  225.7 2.5 %copy-start.3 = (f32[2,768,384]{2,1,0:T(8,128)S(1)}, f32[2,768,384]{2,1,0:T(8,128)}, u32[]{:S(2)}) copy-start(f32[2,768,384]{2,1,0:T(8,128)} %get-tuple-element.46) | copy-start | bytes 7077892
  228.2 2.5 %copy-start.2 = (f32[2,384,768]{2,1,0:T(8,128)S(1)}, f32[2,384,768]{2,1,0:T(8,128)}, u32[]{:S(2)}) copy-start(f32[2,384,768]{2,1,0:T(8,128)} %get-tuple-element.47) | copy-start | bytes 7077892

commit v2 on v1

--- a/solution.py
+++ b/solution.py
@@ -67,7 +67,11 @@
             return 0
         lax.fori_loop(1, N_ROW, row_step, 0)
         count += N_ROW - 1
-    pl.semaphore_wait(barrier, count)
+    return count
+
+
+def all_here(count):
+    pl.semaphore_wait(pltpu.get_barrier_semaphore(), count)
 
 
 def loop(low, high, step):
@@ -75,8 +79,8 @@
 
 
 class Gather:
-    def __init__(self, stage, whole, sems):
-        self.stage, self.whole = stage, whole
+    def __init__(self, begin, stage, whole, sems):
+        self.begin, self.stage, self.whole = begin, stage, whole
         self.s1, self.r1, self.s2, self.r2, self.s3, self.r3 = sems
         self.row, self.col, self.xz, self.core = here()
 
@@ -104,24 +108,21 @@
 
     def start(self, rows):
         self.stage[self.row] = rows
-        loop(1, N_ROW, lambda d: self.first(d).start())
+        self.begin(N_ROW, self.first)
 
     def spread(self):
         loop(1, N_ROW, self.first_arrived)
         block = self.stage[...]
         self.whole[self.core, self.xz] = block.reshape(-1, block.shape[-1]).astype(BF16)
-        loop(1, N_XZ, lambda d: self.second(d).start())
+        self.begin(N_XZ, self.second)
 
     def swap(self):
         loop(1, N_XZ, self.second_arrived)
-        self.third().start()
+        self.begin(2, lambda d: self.third())
 
     def finish(self):
         at = self.whole.at[1 - self.core]
         remote(at, at, self.s3, self.r3, self.row, self.col).wait_recv()
-        loop(1, N_ROW, lambda d: self.first(d).wait_send())
-        loop(1, N_XZ, lambda d: self.second(d).wait_send())
-        self.third().wait_send()
 
 
 def gather_sems():
@@ -135,9 +136,9 @@
     place = core * N_XZ + xz
     y, high = row % 4, row // 4
     other_row = (1 - high) * 4 + y
-    width = n.tok_mean.shape[-1]
+    width = n.tokens.shape[-1]
     units = n.w_gate.shape[-1]
-    capacity = n.rows.shape[2]
+    capacity = n.grid.shape[3]
     slots = N_COL * capacity
     records = N_COL * 8
     batch = N_ROW * records
@@ -148,7 +149,65 @@
     def arrived(at, sem):
         remote(at, at, n.a_send.at[0], sem, row, col).wait_recv()
 
-    greet(True, True)
+    pending = []
+
+    def begin(count, make):
+        loop(1, count, lambda d: make(d).start())
+        pending.append(lambda: loop(1, count, lambda d: make(d).wait_send()))
+
+    def launch(make, *where):
+        make(*where).start()
+        pending.append(lambda: make(*where).wait_send())
+
+    def iota(shape, dim):
+        return lax.broadcasted_iota(jnp.int32, shape, dim)
+
+    def exact(left, right, dims):
+        return lax.dot_general(
+            left, right, (dims, ((), ())), precision=lax.Precision.HIGHEST, preferred_element_type=F32
+        )
+
+    def fast(left, right, dims):
+        return lax.dot_general(left, right, (dims, ((), ())), preferred_element_type=F32)
+
+    def one_hot(at, lanes):
+        return (iota((at.shape[0], lanes), 1) == at).astype(F32)
+
+    greeted = greet(True, True)
+
+    tokens = n.tokens[...].astype(F32)
+    tok_count = tokens.shape[0]
+    inverse_rms = lax.rsqrt(jnp.mean(tokens * tokens, -1, keepdims=True) + 1e-06)
+    norm_in = (tokens * inverse_rms).astype(BF16)
+    scores = exact(norm_in.astype(F32), n.router[...], ((1,), (0,)))
+    experts = scores.shape[-1]
+    ids = [n.ids[:, k : k + 1] for k in range(2)]
+    choose = [one_hot(ids[k], experts) for k in range(2)]
+    chosen = [jnp.sum(choose[k] * scores, -1, keepdims=True) for k in range(2)]
+    gates = [jax.nn.sigmoid(chosen[k] - chosen[1 - k]) for k in range(2)]
+    earlier = (iota((tok_count, tok_count), 0) > iota((tok_count, tok_count), 1)).astype(F32).astype(BF16)
+    before = fast(earlier, (choose[0] + choose[1]).astype(BF16), ((1,), (0,)))
+    to_place, in_line, hits = [], [], []
+    meta = jnp.zeros((N_COL * 8, 128), F32)
+    for k in range(2):
+        position = jnp.sum(choose[k] * before, -1, keepdims=True).astype(jnp.int32)
+        column = ids[k] >> 1
+        to_place.append((column & 1) * N_XZ + (column >> 1))
+        in_line.append((ids[k] & 1) * capacity + position)
+        hits.append(one_hot(to_place[k] * (EXP_DEV * capacity) + in_line[k], N_COL * EXP_DEV * capacity))
+        by_record = one_hot(to_place[k] * 8 + (iota((tok_count, 1), 0) >> 4), N_COL * 8) * gates[k]
+        by_line = one_hot((place % 4) * (EXP_DEV * capacity) + in_line[k], 128)
+        meta = meta + fast(by_record.astype(BF16), by_line.astype(BF16), ((0,), (0,)))
+    hit = (hits[0] + hits[1]).astype(BF16)
+    n.meta[...] = meta.reshape(N_COL, 8, 128)
+    n.rows[...] = fast(hit, norm_in, ((0,), (0,))).astype(BF16).reshape(n.rows.shape)
+    text = n.text[...].astype(F32)
+    text_norm = jnp.sqrt(jnp.sum(text * text, -1, keepdims=True) + 1e-06)
+    text_unit = text / text_norm
+    scale = jnp.exp(jnp.full((8, 128), n.log_scale[0], F32))[:1, :1]
+    shift = n.bias[0]
+    factor = n.loss_scale[0] * scale * (1.0 / batch)
+    all_here(greeted)
 
     def meta_part(d):
         to = (place + d) % N_COL
@@ -160,12 +219,12 @@
             n.rows.at[to], n.grid.at[:, place, row], n.a_send.at[d - 1], n.a_recv.at[place], row, column_of(to)
         )
 
-    loop(1, N_COL, lambda d: meta_part(d).start())
+    begin(N_COL, meta_part)
     own = pltpu.make_async_copy(n.rows.at[place], n.grid.at[:, place, row], n.own_sem)
     own.start()
-    loop(1, N_COL, lambda d: part(d).start())
-    texts = Gather(n.t_stage, n.everyone, [n.ts1, n.tr1, n.ts2, n.tr2, n.ts3, n.tr3])
-    texts.start(n.text[...])
+    begin(N_COL, part)
+    texts = Gather(begin, n.t_stage, n.everyone, [n.ts1, n.tr1, n.ts2, n.tr2, n.ts3, n.tr3])
+    texts.start(text_unit)
     n.table[place] = n.meta[place]
     loop(1, N_COL, lambda d: arrived(n.table.at[(place + N_COL - d) % N_COL], n.m_recv.at[d - 1]))
     n.compact[row] = jnp.sum(n.table[...].reshape(N_COL // 4, 4, 8, 128), 1)
@@ -174,7 +233,7 @@
         at = n.compact.at[row]
         return remote(at, at, n.c_send.at[d - 1], n.c_recv.at[d - 1], (row + d) % N_ROW, col)
 
-    loop(1, N_ROW, lambda d: table_copy(d).start())
+    begin(N_ROW, table_copy)
 
     def piece(ref, group, at_row):
         return ref.at[:, pl.ds(group * PER_GROUP, PER_GROUP), at_row]
@@ -192,9 +251,6 @@
         step = 1 - 2 * way
         at = piece(n.grid, 2 * way + half, row_of(rel, -step))
         return remote(at, at, n.f_send.at[way, rel, half], n.f_recv.at[way, rel, half], row_of(0, step), col)
-
-    def iota(shape, dim):
-        return lax.broadcasted_iota(jnp.int32, shape, dim)
 
     def forward(r):
         def one(x):
@@ -234,23 +290,23 @@
             def _():
                 arrived(n.grid.at[:, from_place, row], n.a_recv.at[from_place])
         loop(0, PER_GROUP, one)
-        across(group).start()
-        near(0, 0, group).start()
-        near(1, 0, group).start()
+        launch(across, group)
+        launch(near, 0, 0, group)
+        launch(near, 1, 0, group)
 
     def neighbour(way, rel, group):
         step = 1 - 2 * way
         arrived(piece(n.grid, group, row_of(rel, -step)), n.n_recv.at[way, rel, group])
         if group // 2 == way:
-            far(way, rel, group % 2).start()
+            launch(far, way, rel, group % 2)
 
     texts.spread()
     forward(row)
     loop(1, N_ROW, lambda d: arrived(n.compact.at[(row + N_ROW - d) % N_ROW], n.c_recv.at[d - 1]))
     for group in range(GROUPS):
         arrived(piece(n.grid, group, other_row), n.x_recv.at[group])
-        near(0, 1, group).start()
-        near(1, 1, group).start()
+        launch(near, 0, 1, group)
+        launch(near, 1, 1, group)
         neighbour(0, 0, group)
         neighbour(1, 0, group)
     texts.swap()
@@ -296,7 +352,7 @@
         to = (xz + d) % N_XZ
         return remote(n.sums.at[to], n.from_xz.at[d - 1], n.s2.at[d - 1], n.r2.at[d - 1], row, to * 2 + core)
 
-    loop(1, N_XZ, lambda d: to_chip(d).start())
+    begin(N_XZ, to_chip)
     loop(1, N_XZ, lambda d: to_chip(d).wait_recv())
     total = n.sums[xz].astype(F32)
     for d in range(N_XZ - 1):
@@ -307,20 +363,20 @@
         to = (row + d) % N_ROW
         return remote(n.sums_row.at[to], n.from_row.at[d - 1], n.s3.at[d - 1], n.r3.at[d - 1], to, col)
 
-    loop(1, N_ROW, lambda d: to_row(d).start())
+    begin(N_ROW, to_row)
     texts.finish()
     loop(1, N_ROW, lambda d: to_row(d).wait_recv())
     total = n.sums_row[row]
     for d in range(N_ROW - 1):
         total = total + n.from_row[d]
-    pooled = n.tok_mean[...] + total * (1.0 / SEQ)
+    tok_mean = jnp.mean(n.tokens[...].astype(F32).reshape(-1, SEQ, width), 1)
+    pooled = tok_mean + total * (1.0 / SEQ)
     pooled_norm = jnp.sqrt(jnp.sum(pooled * pooled, -1, keepdims=True) + 1e-06)
     embed = pooled / pooled_norm
     embed_b = embed.astype(BF16)
-    embeds = Gather(n.e_stage, n.e_whole, [n.es1, n.er1, n.es2, n.er2, n.es3, n.er3])
-    grads = Gather(n.g_stage, n.grads, [n.gs1, n.gr1, n.gs2, n.gr2, n.gs3, n.gr3])
+    embeds = Gather(begin, n.e_stage, n.e_whole, [n.es1, n.er1, n.es2, n.er2, n.es3, n.er3])
+    grads = Gather(begin, n.g_stage, n.grads, [n.gs1, n.gr1, n.gs2, n.gr2, n.gs3, n.gr3])
     embeds.start(embed_b.astype(F32))
-    scale, shift, factor = n.scalars[0], n.scalars[1], n.scalars[2]
     at = (8, batch)
     same = (place * N_ROW + row) * 8 + iota(at, 0) == iota(at, 1)
     labels = jnp.where(same, 1.0, -1.0).astype(F32)
@@ -405,15 +461,15 @@
         backward(row_of(rel, 2))
         for half in range(2):
             for way in range(2):
-                far_back(way, rel, half).start()
+                launch(far_back, way, rel, half)
     for rel in (1, 0):
         loop(0, 2, lambda way, rel=rel: backward(row_of(rel, 1 - 2 * way)))
         for half in range(2):
             for way in range(2):
-                near_back(way, rel, 2 * (1 - way) + half).start()
+                launch(near_back, way, rel, 2 * (1 - way) + half)
     backward(other_row)
     backward(row)
-    loop(1, N_ROW, lambda d: q_row(d).start())
+    begin(N_ROW, q_row)
     embeds.spread()
     for rel in (1, 0):
         for half in range(2):
@@ -421,7 +477,7 @@
                 far_back(way, rel, half).wait_recv()
                 at = n.far_buf.at[way, rel, half]
                 add_into(at, at, piece(n.back, 2 * way + half, row_of(rel, 1 - 2 * way)))
-                near_back(way, rel, 2 * way + half).start()
+                launch(near_back, way, rel, 2 * way + half)
     loop(1, N_ROW, lambda d: q_row(d).wait_recv())
     total = n.q[row]
     for d in range(N_ROW - 1):
@@ -433,7 +489,7 @@
         to = (place + d) % N_COL
         return remote(n.q_msg.at[to], n.q_in.at[place], n.q2_send.at[d - 1], n.q2_recv.at[d - 1], row, column_of(to))
 
-    loop(1, N_COL, lambda d: q_col(d).start())
+    begin(N_COL, q_col)
     embeds.swap()
 
     def weight_grads(x):
@@ -454,24 +510,15 @@
 
     weight_grads(0)
     loop(1, N_COL, lambda d: arrived(n.q_in.at[(place + N_COL - d) % N_COL], n.q2_recv.at[d - 1]))
-    ids = n.ids[...]
-    gates = n.gates[...]
     found = []
     for k in range(2):
-        at = (ids.shape[0], N_COL)
-        by_place = (iota(at, 1) == ids[:, k : k + 1]).astype(F32)
-        lines = jnp.dot(by_place, n.q_in[:, 0, :], precision=lax.Precision.HIGHEST, preferred_element_type=F32)
-        at = (ids.shape[0], 128)
-        found.append(jnp.sum(jnp.where(iota(at, 1) == ids[:, 2 + k : 3 + k], lines, 0.0), -1, keepdims=True))
+        lines = exact(one_hot(to_place[k], N_COL), n.q_in[:, 0, :], ((1,), (0,)))
+        found.append(jnp.sum(one_hot(in_line[k], 128) * lines, -1, keepdims=True))
     both = found[0] + found[1]
-    score_grad = jnp.zeros((ids.shape[0], 128), F32)
+    score_grad = jnp.zeros((tok_count, 128), F32)
     for k in range(2):
-        logit_grad = found[k] - gates[:, k : k + 1] * both
-        score_grad = score_grad + jnp.where(iota(score_grad.shape, 1) == ids[:, 4 + k : 5 + k], logit_grad, 0.0)
-    n.score_grad[...] = score_grad
-    router_part = jnp.dot(
-        score_grad.T[: EXP_DEV * N_COL], n.norm[...], precision=lax.Precision.HIGHEST, preferred_element_type=F32
-    )
+        score_grad = score_grad + one_hot(ids[k], 128) * (found[k] - gates[k] * both)
+    router_part = exact(score_grad.T[:experts], norm_in.astype(F32), ((1,), (0,)))
     for i in range(4):
         for j in range(2):
             n.dr[j * 4 + i] = router_part[i * 8 : i * 8 + 8, j * (width // 2) : (j + 1) * (width // 2)]
@@ -485,20 +532,20 @@
         return remote(at, at, n.d2_send.at[d - 1], n.d2_recv.at[d - 1], row, (col + d) % N_COL)
 
     def tell_row(d):
-        at = n.d_router.at[row]
+        at = n.dr_out.at[row]
         return remote(at, at, n.d3_send.at[d - 1], n.d3_recv.at[d - 1], (row + d) % N_ROW, col)
 
-    loop(1, N_ROW, lambda d: scatter(d).start())
+    begin(N_ROW, scatter)
     n.dr_in[row] = n.dr[row]
     for group in (2, 0, 3, 1):
         for way in range(2):
             near_back(way, 1, group).wait_recv()
         at = n.near_buf.at[0, 1, group]
         add_into(at, at, n.near_buf.at[1, 1, group], piece(n.back, group, other_row))
-        across_back(group).start()
+        launch(across_back, group)
     loop(1, N_ROW, lambda d: arrived(n.dr_in.at[(row + N_ROW - d) % N_ROW], n.d1_recv.at[d - 1]))
     n.dr_sum[col] = jnp.sum(n.dr_in[...], 0)
-    loop(1, N_COL, lambda d: tell_col(d).start())
+    begin(N_COL, tell_col)
     weight_grads(1)
 
     def down_grads(x):
@@ -514,12 +561,11 @@
     down_grads(0)
     down_grads(1)
     loop(1, N_COL, lambda d: arrived(n.dr_sum.at[(col + N_COL - d) % N_COL], n.d2_recv.at[d - 1]))
-    n.d_router[row] = jnp.sum(n.dr_sum[...], 0)
-    loop(1, N_ROW, lambda d: tell_row(d).start())
+    n.dr_out[row] = jnp.sum(n.dr_sum[...], 0)
+    begin(N_ROW, tell_row)
     embeds.finish()
-    text_unit = n.text[...]
     text_grad = weigh(text_unit.astype(BF16), n.e_whole[...].reshape(batch, width))
-    n.d_text[...] = (text_grad - text_unit * jnp.sum(text_unit * text_grad, -1, keepdims=True)) / n.text_norm[...]
+    n.d_text[...] = (text_grad - text_unit * jnp.sum(text_unit * text_grad, -1, keepdims=True)) / text_norm
 
     def home(group, i):
         to = group * PER_GROUP + i
@@ -549,29 +595,9 @@
                 own_home(group, i).start()
         loop(0, PER_GROUP, send)
 
-    loop(1, N_ROW, lambda d: arrived(n.d_router.at[(row + N_ROW - d) % N_ROW], n.d3_recv.at[d - 1]))
-    loop(1, N_COL, lambda d: meta_part(d).wait_send())
-    loop(1, N_COL, lambda d: part(d).wait_send())
-    loop(1, N_COL, lambda d: q_col(d).wait_send())
-    loop(1, N_COL, lambda d: tell_col(d).wait_send())
-    loop(1, N_ROW, lambda d: table_copy(d).wait_send())
-    loop(1, N_ROW, lambda d: to_row(d).wait_send())
-    loop(1, N_ROW, lambda d: q_row(d).wait_send())
-    loop(1, N_ROW, lambda d: scatter(d).wait_send())
-    loop(1, N_ROW, lambda d: tell_row(d).wait_send())
-    loop(1, N_XZ, lambda d: to_chip(d).wait_send())
-    for group in range(GROUPS):
-        across(group).wait_send()
-        across_back(group).wait_send()
-        for way in range(2):
-            for rel in range(2):
-                near(way, rel, group).wait_send()
-                near_back(way, rel, group).wait_send()
-    for rel in range(2):
-        for half in range(2):
-            for way in range(2):
-                far(way, rel, half).wait_send()
-                far_back(way, rel, half).wait_send()
+    loop(1, N_ROW, lambda d: arrived(n.dr_out.at[(row + N_ROW - d) % N_ROW], n.d3_recv.at[d - 1]))
+    for wait in pending:
+        wait()
     for x in range(EXP_DEV):
         pltpu.make_async_copy(n.gate_out.at[x], n.d_gate.at[x], n.out_sem.at[0, x]).wait()
         pltpu.make_async_copy(n.up_out.at[x], n.d_up.at[x], n.out_sem.at[1, x]).wait()
@@ -584,28 +610,42 @@
             def _():
                 home(group, i).wait_send()
         loop(0, PER_GROUP, sent)
+    for j in range(2):
+        block = n.dr_out[pl.ds(j * 4, 4)].reshape(experts, width // 2)
+        block = jnp.concatenate([block, jnp.zeros((128 - experts, width // 2), F32)], 0)
+        n.d_router[pl.ds(j * (width // 2), width // 2), :] = block.T[:, :experts]
+    input_sum = fast(hit, n.slots[...].reshape(-1, width), ((1,), (0,)))
+    norm_grad = input_sum + exact(score_grad[:, :experts], n.router[...], ((1,), (1,)))
+    normed = n.tokens[...].astype(F32) * inverse_rms
+    out_grad = jnp.broadcast_to(n.own_grad[...][:, None, :], (8, SEQ, width)).reshape(tok_count, width)
+    n.d_tokens[...] = out_grad + inverse_rms * (
+        norm_grad - normed * jnp.mean(norm_grad * normed, -1, keepdims=True)
+    )
 
 
 def fused(ins):
-    width = ins["tok_mean"].shape[-1]
+    tok_count, width = ins["tokens"].shape
     units = ins["w_gate"].shape[-1]
-    tok_count = ins["ids"].shape[0]
-    capacity = ins["rows"].shape[2]
+    experts = EXP_DEV * N_COL
+    capacity = max(2, 4 * tok_count // experts)
     slots, records = N_COL * capacity, N_COL * 8
     whole = (2, N_XZ, N_ROW * 8, width)
     block = (EXP_DEV, PER_GROUP, capacity, width)
     grid = (EXP_DEV, N_COL, N_ROW, capacity)
     outs = {
-        "own_grad": ((8, width), F32, VMEM),
         "d_text": ((8, width), F32, VMEM),
-        "slots": ((N_COL, EXP_DEV, capacity, width), BF16, VMEM),
-        "score_grad": ((tok_count, 128), F32, VMEM),
-        "d_router": ((N_ROW, 8, width // 2), F32, VMEM),
+        "d_tokens": ((tok_count, width), F32, VMEM),
         "d_gate": (ins["w_gate"].shape, F32, ANY),
         "d_up": (ins["w_up"].shape, F32, ANY),
         "d_down": (ins["w_down"].shape, F32, ANY),
+        "d_router": (ins["router"].shape, F32, VMEM),
     }
     scratch = {
+        "rows": ((N_COL, EXP_DEV, capacity, width), BF16),
+        "meta": ((N_COL, 8, 128), F32),
+        "own_grad": ((8, width), F32),
+        "slots": ((N_COL, EXP_DEV, capacity, width), BF16),
+        "dr_out": ((N_ROW, 8, width // 2), F32),
         "grid": (grid + (width,), BF16),
         "table": ((N_COL, 8, 128), F32),
         "compact": ((N_ROW, N_COL // 4, 8, 128), F32),
@@ -662,7 +702,7 @@
     result = pl.pallas_call(
         functools.partial(fused_kernel, names),
         out_shape=tuple(jax.ShapeDtypeStruct(shape, dtype) for shape, dtype, _ in outs.values()),
-        in_specs=[SMEM if name == "scalars" else VMEM for name in ins],
+        in_specs=[SMEM if name in ("log_scale", "bias", "loss_scale") else VMEM for name in ins],
         out_specs=tuple(spec for _, _, spec in outs.values()),
         scratch_shapes=[pltpu.VMEM(shape, dtype) for shape, dtype in scratch.values()]
         + [pltpu.SemaphoreType.DMA(shape) for shape in sems.values()],
@@ -670,72 +710,14 @@
             collective_id=0, has_side_effects=True, vmem_limit_bytes=61 << 20
         ),
     )(*ins.values())
-    return dict(zip(outs, result))
+    return result
 
 
 def body(tokens, expert_ids, text, w_gate, w_up, w_down, router, log_scale, bias, loss_scale):
-    tok_count, width = tokens.shape
-    samples = tok_count // SEQ
-    experts = EXP_DEV * N_COL
-    capacity = max(2, 4 * tok_count // experts)
-    line = EXP_DEV * capacity
-    batch = samples * N_ROW * N_COL
-    token_wide = tokens.astype(F32)
-    inverse_rms = lax.rsqrt(jnp.mean(token_wide * token_wide, -1, keepdims=True) + 1e-06)
-    normed = token_wide * inverse_rms
-    norm_in = normed.astype(BF16)
-    norm_wide = norm_in.astype(F32)
-    scores = jnp.dot(norm_wide, router, precision=lax.Precision.HIGHEST)
-    choose = (expert_ids[:, :, None] == jnp.arange(experts, dtype=jnp.int32)[None, None, :]).astype(F32)
-    chosen = jnp.sum(choose * scores[:, None, :], -1)
-    gates = jax.nn.sigmoid(chosen - chosen[:, ::-1])
-    member = jnp.sum(choose, 1)
-    before = jnp.cumsum(member, 0) - member
-    position = jnp.sum(choose * before[:, None, :], -1).astype(jnp.int32)
-    to_place = place_of(expert_ids // EXP_DEV)
-    in_line = (expert_ids % EXP_DEV) * capacity + position
-    slot_index = to_place * line + in_line
-    slot = jnp.arange(experts * capacity, dtype=jnp.int32)[:, None]
-    hit0 = slot_index[:, 0][None, :] == slot
-    hit1 = slot_index[:, 1][None, :] == slot
-    both = (hit0 | hit1).astype(BF16)
-    outgoing = jnp.dot(both, norm_in, preferred_element_type=F32).astype(BF16)
-    slot_gate = jnp.sum(
-        jnp.where(hit0, gates[:, 0][None, :], 0.0) + jnp.where(hit1, gates[:, 1][None, :], 0.0), -1
-    )
-    record = (jnp.arange(tok_count, dtype=jnp.int32) // SEQ)[None, :]
-    slot_record = jnp.sum(jnp.where(hit0 | hit1, record, 0), -1)
-    in_record = slot_record.reshape(N_COL, 1, line) == jnp.arange(samples, dtype=jnp.int32)[None, :, None]
-    meta = jnp.where(in_record, slot_gate.reshape(N_COL, 1, line), 0.0)
-    own_place = place_of(lax.axis_index("col"))
-    mine = (jnp.arange(128, dtype=jnp.int32) // line == own_place % 4)[None, None, :]
-    meta = jnp.where(mine, jnp.tile(meta, (1, 1, 128 // line)), 0.0)
-    text_wide = text.astype(F32)
-    text_norm = jnp.sqrt(jnp.sum(text_wide * text_wide, -1, keepdims=True) + 1e-06)
-    scale = jnp.exp(log_scale[0])
-    got = fused({
-        "scalars": jnp.stack([scale, bias[0], loss_scale[0] * scale / batch]),
-        "rows": outgoing.reshape(N_COL, EXP_DEV, capacity, width),
-        "meta": meta,
-        "text": text_wide / text_norm,
-        "text_norm": text_norm,
-        "tok_mean": jnp.mean(token_wide.reshape(samples, SEQ, width), 1),
-        "w_gate": w_gate,
-        "w_up": w_up,
-        "w_down": w_down,
-        "ids": jnp.concatenate([to_place, in_line, expert_ids, expert_ids], -1),
-        "gates": gates,
-        "norm": norm_wide,
+    return fused({
+        "tokens": tokens, "ids": expert_ids, "text": text, "w_gate": w_gate, "w_up": w_up, "w_down": w_down,
+        "router": router, "log_scale": log_scale, "bias": bias, "loss_scale": loss_scale,
     })
-    input_sum = lax.dot_general(
-        both, got["slots"].reshape(-1, width), (((0,), (0,)), ((), ())), preferred_element_type=F32
-    )
-    score_grad = got["score_grad"][:, :experts]
-    out_grad = jnp.repeat(got["own_grad"], SEQ, axis=0)
-    norm_grad = input_sum + jnp.dot(score_grad, router.T, precision=lax.Precision.HIGHEST)
-    d_tokens = out_grad + inverse_rms * (norm_grad - normed * jnp.mean(norm_grad * normed, -1, keepdims=True))
-    d_router = got["d_router"].reshape(2, experts, width // 2).transpose(0, 2, 1).reshape(width, experts)
-    return (got["d_text"], d_tokens, got["d_gate"], got["d_up"], got["d_down"], d_router)
 
 
 def solution(mesh):

time: 233 us -> 220 us (0.944)
  other arithmetic: 10.7 us -> 0 us
  matrix products: 5.44 us -> 0 us
  local copies, waits for them, and re-layouts: 11.1 us -> 15.4 us
    unnamed x20 -> x11, local copies, waits for them, and re-layouts: 7.08 us -> 13.6 us
    dot_general x4 -> x0, matrix products: 5.44 us -> none  [the longest x1 1.45 us: body(): lax.dot_general(both, got['slots'].reshape(-1, width), (((0,), (0,)), (()...]
    reduce_sum x7 -> x0, other arithmetic: 4.62 us -> none  [the longest x1 1.05 us: body(): jnp.mean(token_wide * token_wide, -1, keepdims=True) + 1e-06]
where the time goes in v2:
time: 220 us; the launch traced here: 219 us
  Pallas kernels  201 us (91%)
  local copies, waits for them, and re-layouts  15.4 us (7%)
  between operations  2.58 us (1%)
    pallas_call x1, Pallas kernels, fused(): pl.pallas_call(functools.partial(fused_kernel, names), out_shape=tuple((j...  201 us
    unnamed x11, local copies, waits for them, and re-layouts  13.6 us

profile of v2, /device:TPU:1, one launch (start us, length us, event | category | flops | bytes accessed | tf_op | source)
XLA Modules:
  0.0 219.2 jit_solution(199800760177275082)
XLA Ops:
  2.6 1.4 copy.16.refs_1_
  4.0 1.8 copy.17.refs_6_
  5.8 201.2 %shard_map.145 = (f32[8,768]{1,0:T(8,128)}, f32[128,768]{1,0:T(8,128)}, f32[2,768,384]{2,1,0:T(8,128)}, f32[2,768,384]{2,1,0:T(8,128)}, f32[2,384,768]{2,1,0:T(8,128)}, /*index=5*/f32[768,32]{1,0:T(8,128)}) custom-call(bf16[128,768]{1,0:T(8,128)(2,1)} %refs_0_.1, s32[128,2]{1,0:T(8,128)} %copy.16.refs_1_, bf16[8,768]{1,0:T(8,128)(2,1)} %refs_2_.1, ...), custom_call_target="tpu_custom_call" | custom-call | tf_op jit(solution)/shard_map/pallas_call | solution.py:702
  207.0 1.8 copy.18
  208.7 1.3 copy.27
  210.1 1.8 copy.28
  211.9 0.0 copy-start.1
  211.9 3.4 %copy.29 = f32[2,768,384]{2,1,0:T(8,128)} copy(f32[2,768,384]{2,1,0:T(8,128)} %get-tuple-element.20) | data formatting | bytes 4718592
  215.2 0.0 copy-done.1
  215.2 0.0 copy-start
  215.2 1.4 copy.30
  216.6 1.1 copy-done
  217.8 1.4 copy.31
Async XLA Ops:
  211.9 3.4 %copy-start.1 = (f32[2,768,384]{2,1,0:T(8,128)S(1)}, f32[2,768,384]{2,1,0:T(8,128)}, u32[]{:S(2)}) copy-start(f32[2,768,384]{2,1,0:T(8,128)} %get-tuple-element.21) | copy-start | bytes 7077892
  215.2 2.5 %copy-start = (f32[2,384,768]{2,1,0:T(8,128)S(1)}, f32[2,384,768]{2,1,0:T(8,128)}, u32[]{:S(2)}) copy-start(f32[2,384,768]{2,1,0:T(8,128)} %get-tuple-element.22) | copy-start | bytes 7077892

commit v3 on v2

v3 whole, which is shorter than its diff:
```python
import functools
import types

import jax
import jax.numpy as jnp
from jax import lax
from jax.experimental import pallas as pl
from jax.experimental.pallas import tpu as pltpu
from jax.sharding import PartitionSpec as P

EXP_DEV = 2
SEQ = 16
F32 = jnp.float32
BF16 = jnp.bfloat16
MESH = pl.DeviceIdType.MESH
VMEM = pl.BlockSpec(memory_space=pltpu.VMEM)
SMEM = pl.BlockSpec(memory_space=pltpu.SMEM)
ANY = pl.BlockSpec(memory_space=pl.ANY)
N_ROW, N_COL, N_XZ = 8, 16, 8
X_OUT, X_BACK = 9, 8
KEPT = ("d_gate", "d_up", "d_down", "d_text", "d_tokens", "d_router")


def column_of(place):
    return (place % N_XZ) * 2 + place // N_XZ


def place_of(column):
    return (column % 2) * N_XZ + column // 2


def remote(src, dst, send_sem, recv_sem, row, col):
    return pltpu.make_async_remote_copy(
        src_ref=src, dst_ref=dst, send_sem=send_sem, recv_sem=recv_sem,
        device_id={"row": row, "col": col}, device_id_type=MESH,
    )


def here():
    row, col = lax.axis_index("row"), lax.axis_index("col")
    return row, col, col // 2, col % 2


def greet(all_columns, all_rows):
    row, col, xz, core = here()
    barrier = pltpu.get_barrier_semaphore()

    def signal(r, c):
        pl.semaphore_signal(barrier, inc=1, device_id={"row": r, "col": c}, device_id_type=MESH)

    count = 0
    if all_columns:
        def col_step(d, _):
            signal(row, (col + d) % N_COL)
            return 0
        lax.fori_loop(1, N_COL, col_step, 0)
        count += N_COL - 1
    else:
        def xz_step(d, _):
            signal(row, ((xz + d) % N_XZ) * 2 + core)
            return 0
        lax.fori_loop(1, N_XZ, xz_step, 0)
        signal(row, xz * 2 + 1 - core)
        count += N_XZ
    if all_rows:
        def row_step(d, _):
            signal((row + d) % N_ROW, col)
            return 0
        lax.fori_loop(1, N_ROW, row_step, 0)
        count += N_ROW - 1
    return count


def all_here(count):
    pl.semaphore_wait(pltpu.get_barrier_semaphore(), count)


def loop(low, high, step):
    lax.fori_loop(low, high, lambda i, _: (step(i), 0)[1], 0)


class Gather:
    def __init__(self, begin, stage, whole, sems):
        self.begin, self.stage, self.whole = begin, stage, whole
        self.s1, self.r1, self.s2, self.r2, self.s3, self.r3 = sems
        self.row, self.col, self.xz, self.core = here()

    def first(self, d):
        to = (self.row + d) % N_ROW
        mine = self.stage.at[self.row]
        return remote(mine, mine, self.s1.at[d - 1], self.r1.at[d - 1], to, self.col)

    def second(self, d):
        to = (self.xz + d) % N_XZ
        mine = self.whole.at[self.core, self.xz]
        return remote(mine, mine, self.s2.at[d - 1], self.r2.at[d - 1], self.row, to * 2 + self.core)

    def third(self, d):
        at = self.whole.at[self.core, (self.xz + N_XZ - d) % N_XZ]
        return remote(at, at, self.s3.at[d], self.r3.at[d], self.row, self.xz * 2 + 1 - self.core)

    def first_arrived(self, d):
        at = self.stage.at[(self.row + N_ROW - d) % N_ROW]
        remote(at, at, self.s1.at[d - 1], self.r1.at[d - 1], self.row, self.col).wait_recv()

    def second_arrived(self, d):
        at = self.whole.at[self.core, (self.xz + N_XZ - d) % N_XZ]
        remote(at, at, self.s2.at[d - 1], self.r2.at[d - 1], self.row, self.col).wait_recv()

    def start(self, rows):
        self.stage[self.row] = rows
        self.begin(N_ROW, self.first)

    def spread(self):
        loop(1, N_ROW, self.first_arrived)
        block = self.stage[...]
        self.whole[self.core, self.xz] = block.reshape(-1, block.shape[-1]).astype(BF16)
        self.begin(N_XZ, self.second)
        self.third(0).start()

    def swap(self):
        def one(d):
            self.second_arrived(d)
            self.third(d).start()
        loop(1, N_XZ, one)

    def finish(self):
        def one(d):
            at = self.whole.at[1 - self.core, (self.xz + N_XZ - d) % N_XZ]
            remote(at, at, self.s3.at[d], self.r3.at[d], self.row, self.col).wait_recv()
        loop(0, N_XZ, one)
        loop(0, N_XZ, lambda d: self.third(d).wait_send())


class QuietGather(Gather):
    def __init__(self, begin, stage, whole, sems):
        super().__init__(begin, stage, whole, sems[:6])
        self.s4, self.r4 = sems[6:]
        self.x, self.z = self.xz // 4, self.xz % 4

    def column(self, x, z, core):
        return (x * 4 + z) * 2 + core

    def pair(self):
        at = self.whole.at[self.core, self.x, self.z]
        return remote(at, at, self.s4, self.r4, self.row, self.column(1 - self.x, self.z, self.core))

    def second(self, d):
        at = self.whole.at[self.core, :, self.z]
        to = self.column(self.x, (self.z + d) % 4, self.core)
        return remote(at, at, self.s2.at[d - 1], self.r2.at[d - 1], self.row, to)

    def third(self, d):
        at = self.whole.at[self.core, :, (self.z + 4 - d) % 4]
        return remote(at, at, self.s3.at[d], self.r3.at[d], self.row, self.xz * 2 + 1 - self.core)

    def spread(self):
        loop(1, N_ROW, self.first_arrived)
        block = self.stage[...]
        self.whole[self.core, self.x, self.z] = block.reshape(-1, block.shape[-1]).astype(BF16)
        self.begin(2, lambda d: self.pair())

    def relay(self):
        at = self.whole.at[self.core, 1 - self.x, self.z]
        remote(at, at, self.s4, self.r4, self.row, self.col).wait_recv()
        self.begin(4, self.second)
        self.third(0).start()

    def swap(self):
        def one(d):
            at = self.whole.at[self.core, :, (self.z + 4 - d) % 4]
            remote(at, at, self.s2.at[d - 1], self.r2.at[d - 1], self.row, self.col).wait_recv()
            self.third(d).start()
        loop(1, 4, one)

    def finish(self):
        def one(d):
            at = self.whole.at[1 - self.core, :, (self.z + 4 - d) % 4]
            remote(at, at, self.s3.at[d], self.r3.at[d], self.row, self.col).wait_recv()
        loop(0, 4, one)
        loop(0, 4, lambda d: self.third(d).wait_send())


def fused_kernel(names, *refs):
    n = types.SimpleNamespace(**dict(zip(names, refs)))
    row, col, xz, core = here()
    place = core * N_XZ + xz
    y, high = row % 4, row // 4
    other_row = (1 - high) * 4 + y
    width = n.tokens.shape[-1]
    units = n.w_gate.shape[-1]
    capacity = n.grid.shape[3]
    slots = N_COL * capacity
    records = N_COL * 8
    batch = N_ROW * records

    def row_of(rel, step):
        return ((high + rel) % 2) * 4 + (y + step + 4) % 4

    def arrived(at, sem):
        remote(at, at, n.a_send.at[0], sem, row, col).wait_recv()

    pending = []

    def begin(count, make):
        loop(1, count, lambda d: make(d).start())
        pending.append(lambda: loop(1, count, lambda d: make(d).wait_send()))

    def iota(shape, dim):
        return lax.broadcasted_iota(jnp.int32, shape, dim)

    def exact(left, right, dims):
        return lax.dot_general(
            left, right, (dims, ((), ())), precision=lax.Precision.HIGHEST, preferred_element_type=F32
        )

    def fast(left, right, dims):
        return lax.dot_general(left, right, (dims, ((), ())), preferred_element_type=F32)

    def one_hot(at, lanes):
        return (iota((at.shape[0], lanes), 1) == at).astype(F32)

    greeted = greet(True, True)

    tokens = n.tokens[...].astype(F32)
    tok_count = tokens.shape[0]
    inverse_rms = lax.rsqrt(jnp.mean(tokens * tokens, -1, keepdims=True) + 1e-06)
    norm_in = (tokens * inverse_rms).astype(BF16)
    scores = exact(norm_in.astype(F32), n.router[...], ((1,), (1,)))
    experts = scores.shape[-1]
    diagonal = iota((tok_count, tok_count), 0) == iota((tok_count, tok_count), 1)
    ids = [jnp.sum(jnp.where(diagonal, n.ids[k : k + 1], 0), -1, keepdims=True) for k in range(2)]
    choose = [one_hot(ids[k], experts) for k in range(2)]
    chosen = [jnp.sum(choose[k] * scores, -1, keepdims=True) for k in range(2)]
    gates = [jax.nn.sigmoid(chosen[k] - chosen[1 - k]) for k in range(2)]
    earlier = (iota((tok_count, tok_count), 0) > iota((tok_count, tok_count), 1)).astype(F32).astype(BF16)
    before = fast(earlier, (choose[0] + choose[1]).astype(BF16), ((1,), (0,)))
    to_place, in_line, hits = [], [], []
    meta = jnp.zeros((N_COL * 8, 128), F32)
    for k in range(2):
        position = jnp.sum(choose[k] * before, -1, keepdims=True).astype(jnp.int32)
        column = ids[k] >> 1
        to_place.append((column & 1) * N_XZ + (column >> 1))
        in_line.append((ids[k] & 1) * capacity + position)
        hits.append(one_hot(to_place[k] * (EXP_DEV * capacity) + in_line[k], N_COL * EXP_DEV * capacity))
        by_record = one_hot(to_place[k] * 8 + (iota((tok_count, 1), 0) >> 4), N_COL * 8) * gates[k]
        by_line = one_hot((place % 4) * (EXP_DEV * capacity) + in_line[k], 128)
        meta = meta + fast(by_record.astype(BF16), by_line.astype(BF16), ((0,), (0,)))
    hit = (hits[0] + hits[1]).astype(BF16)
    n.meta[...] = meta.reshape(N_COL, 8, 128)
    n.rows[...] = fast(hit, norm_in, ((0,), (0,))).astype(BF16).reshape(n.rows.shape)
    text = n.text[...].astype(F32)
    text_norm = jnp.sqrt(jnp.sum(text * text, -1, keepdims=True) + 1e-06)
    text_unit = text / text_norm
    scale = jnp.exp(jnp.full((8, 128), n.log_scale[0], F32))[:1, :1]
    shift = n.bias[0]
    factor = n.loss_scale[0] * scale * (1.0 / batch)
    all_here(greeted)

    def meta_part(d):
        to = (place + d) % N_COL
        return remote(n.meta.at[to], n.table.at[place], n.m_send.at[d - 1], n.m_recv.at[d - 1], row, column_of(to))

    def part(d):
        to = (place + d) % N_COL
        return remote(
            n.rows.at[to], n.grid.at[:, place, row], n.a_send.at[d - 1], n.a_recv.at[place], row, column_of(to)
        )

    begin(N_COL, meta_part)
    own = pltpu.make_async_copy(n.rows.at[place], n.grid.at[:, place, row], n.own_sem)
    own.start()
    begin(N_COL, part)
    texts = QuietGather(
        begin, n.t_stage, n.everyone, [n.ts1, n.tr1, n.ts2, n.tr2, n.ts3, n.tr3, n.ts4, n.tr4]
    )
    texts.start(text_unit)
    n.table[place] = n.meta[place]
    loop(1, N_COL, lambda d: arrived(n.table.at[(place + N_COL - d) % N_COL], n.m_recv.at[d - 1]))
    n.compact[row] = jnp.sum(n.table[...].reshape(N_COL // 4, 4, 8, 128), 1)

    def table_copy(d):
        at = n.compact.at[row]
        return remote(at, at, n.c_send.at[d - 1], n.c_recv.at[d - 1], (row + d) % N_ROW, col)

    begin(N_ROW, table_copy)

    def near_of(way):
        return 1 - 2 * way

    def source(d):
        return (place + N_COL - d) % N_COL

    def block(d, at_row):
        return n.grid.at[:, source(d), at_row]

    def across(step, d):
        at = block(d, row_of(0, step))
        return remote(at, at, n.x_send.at[step % 4, d], n.x_recv.at[step % 4, d], other_row, col)

    def near(way, rel, d):
        at = block(d, row_of(rel, 0))
        return remote(at, at, n.n_send.at[way, rel, d], n.n_recv.at[way, rel, d], row_of(0, near_of(way)), col)

    def far(rel, d):
        step = near_of(d % 2)
        at = block(d, row_of(rel, -step))
        return remote(at, at, n.f_send.at[rel, d], n.f_recv.at[rel, d], row_of(0, step), col)

    def got_across(step, d):
        arrived(block(d, row_of(1, step)), n.x_recv.at[step % 4, d])

    def got_near(way, rel, d):
        arrived(block(d, row_of(rel, -near_of(way))), n.n_recv.at[way, rel, d])

    def got_far(rel, d):
        arrived(block(d, row_of(rel, 2)), n.f_recv.at[rel, d])

    def forward(r):
        def one(x):
            tile = n.compact[r]
            spread = jnp.broadcast_to(tile[:, None], (4, 4, 8, 128)).reshape(records, 128)
            at = (records, 128)
            spread = jnp.where(iota(at, 1) // 32 == (iota(at, 0) // 8) % 4, spread, 0.0).astype(BF16)
            at = (128, slots)
            pick = (iota(at, 0) % 32 == x * capacity + iota(at, 1) % capacity).astype(F32).astype(BF16)
            at = (records, slots)
            pool = jnp.dot(spread, pick, preferred_element_type=F32)
            pool = jnp.where(iota(at, 0) // 8 == iota(at, 1) // capacity, pool, 0.0).astype(BF16)
            at = (slots, 128)
            pick = (iota(at, 1) % 32 == x * capacity + iota(at, 0) % capacity).astype(F32).astype(BF16)
            at = (slots, records)
            turned = lax.dot_general(pick, spread, (((1,), (1,)), ((), ())), preferred_element_type=F32)
            n.turned[r, x] = jnp.where(iota(at, 1) // 8 == iota(at, 0) // capacity, turned, 0.0).astype(BF16)
            rows = n.grid[x, :, r].reshape(slots, width)
            gate_pre = jnp.dot(rows, n.w_gate[x], preferred_element_type=F32)
            up_pre = jnp.dot(rows, n.w_up[x], preferred_element_type=F32)
            sigma = jax.nn.sigmoid(gate_pre)
            silu_gate = gate_pre * sigma
            hidden = (silu_gate * up_pre).astype(BF16)
            shape = (N_COL, capacity, units)
            n.hidden[x, :, r] = hidden.reshape(shape)
            n.for_gate[x, :, r] = (up_pre * (sigma * (1.0 + gate_pre * (1.0 - sigma)))).astype(BF16).reshape(shape)
            n.for_up[x, :, r] = silu_gate.astype(BF16).reshape(shape)
            n.acc[x, :, r] = jnp.dot(pool, hidden, preferred_element_type=F32).reshape(N_COL, 8, units)
        loop(0, EXP_DEV, one)

    def from_column(d):
        @pl.when(d != 0)
        def _():
            arrived(block(d, row), n.a_recv.at[source(d)])

        near(0, 0, d).start()
        near(1, 0, d).start()
        across(0, d).start()

    own.wait()
    loop(0, N_COL, from_column)
    texts.spread()
    forward(row)
    loop(1, N_ROW, lambda d: arrived(n.compact.at[(row + N_ROW - d) % N_ROW], n.c_recv.at[d - 1]))

    def x_first(d):
        got_across(0, d)
        near(0, 1, d).start()
        near(1, 1, d).start()
        got_near(0, 0, d)
        got_near(1, 0, d)
        far(0, d).start()

    def y_first(d):
        got_near(0, 0, d)
        got_near(1, 0, d)
        far(0, d).start()
        across(-1, d).start()
        across(1, d).start()

    def y_first_far(d):
        got_far(0, d)
        across(2, d).start()
        got_across(0, d)

    def x_first_other(d):
        got_near(0, 1, d)
        got_near(1, 1, d)
        far(1, d).start()

    def y_first_other(d):
        got_across(-1, d)
        got_across(1, d)

    loop(0, X_OUT, x_first)
    texts.relay()
    loop(X_OUT, N_COL, y_first)
    loop(0, 2, lambda way: forward(row_of(0, near_of(way))))
    loop(X_OUT, N_COL, y_first_far)
    forward(other_row)
    texts.swap()
    loop(0, X_OUT, x_first_other)
    loop(X_OUT, N_COL, y_first_other)
    loop(0, 2, lambda way: forward(row_of(1, near_of(way))))
    loop(0, X_OUT, lambda d: got_far(0, d))
    forward(row_of(0, 2))
    loop(0, X_OUT, lambda d: got_far(1, d))
    loop(X_OUT, N_COL, lambda d: got_across(2, d))
    forward(row_of(1, 2))

    def sent_first(d):
        far(1, d).wait_send()
        for way in range(2):
            near(way, 1, d).wait_send()

    def sent_all(d):
        far(0, d).wait_send()
        across(0, d).wait_send()
        for way in range(2):
            near(way, 0, d).wait_send()

    def sent_last(d):
        for step in (-1, 1, 2):
            across(step, d).wait_send()

    pending.append(lambda: loop(0, X_OUT, sent_first))
    pending.append(lambda: loop(0, N_COL, sent_all))
    pending.append(lambda: loop(X_OUT, N_COL, sent_last))

    def quarter(q):
        return n.hb[0, q], n.hb[1, q]

    def round_pooled(q):
        for x in range(EXP_DEV):
            n.hb[x, q] = n.acc[x, pl.ds(q * 4, 4)].reshape(-1, units).astype(BF16)

    def shares(k):
        return n.back.at[0, pl.ds(k * 4, 4)]

    def of_chip(first, i):
        return n.back.at[0, first + i // 2, pl.ds((i % 2) * 4, 4)]

    def came(d):
        return n.back.at[1, (d - 1) // 2, pl.ds(((d - 1) % 2) * 4, 4)]

    def share(q):
        first, second = quarter(q)
        total = fast(first, n.w_down[0], ((1,), (0,))) + fast(second, n.w_down[1], ((1,), (0,)))
        n.back[0, pl.ds(q * 2, 2)] = total.astype(BF16).reshape(2, N_ROW, capacity, width)

    loop(0, 4, round_pooled)
    loop(0, 2, lambda i: share((1 - core) * 2 + i))
    swap = remote(shares(1 - core), shares(2), n.s1, n.r1, row, xz * 2 + 1 - core)
    swap.start()
    loop(0, 2, lambda i: share(core * 2 + i))
    swap.wait()

    def add(i):
        of_chip(12, i)[...] = (of_chip(core * 4, i)[...].astype(F32) + of_chip(8, i)[...].astype(F32)).astype(BF16)

    loop(0, N_XZ, add)

    def to_chip(d):
        to = (xz + d) % N_XZ
        return remote(of_chip(12, to), came(d), n.s2.at[d - 1], n.r2.at[d - 1], row, to * 2 + core)

    loop(1, N_XZ, lambda d: to_chip(d).start())
    loop(1, N_XZ, lambda d: to_chip(d).wait_recv())
    total = of_chip(12, xz)[...].astype(F32)
    for d in range(1, N_XZ):
        total = total + came(d)[...].astype(F32)
    n.sums_row[...] = total.reshape(n.sums_row.shape)
    loop(1, N_XZ, lambda d: to_chip(d).wait_send())

    def to_row(d):
        to = (row + d) % N_ROW
        return remote(n.sums_row.at[to], n.from_row.at[d - 1], n.s3.at[d - 1], n.r3.at[d - 1], to, col)

    begin(N_ROW, to_row)
    texts.finish()
    loop(1, N_ROW, lambda d: to_row(d).wait_recv())
    total = n.sums_row[row]
    for d in range(N_ROW - 1):
        total = total + n.from_row[d]
    tok_mean = jnp.mean(n.tokens[...].astype(F32).reshape(-1, SEQ, width), 1)
    pooled = tok_mean + total * (1.0 / SEQ)
    pooled_norm = jnp.sqrt(jnp.sum(pooled * pooled, -1, keepdims=True) + 1e-06)
    embed = pooled / pooled_norm
    embed_b = embed.astype(BF16)
    embeds = QuietGather(
        begin, n.e_stage, n.e_whole, [n.es1, n.er1, n.es2, n.er2, n.es3, n.er3, n.es4, n.er4]
    )
    grads = Gather(begin, n.g_stage, n.grads, [n.gs1, n.gr1, n.gs2, n.gr2, n.gs3, n.gr3])
    embeds.start(embed_b.astype(F32))
    at = (8, batch)
    same = (place * N_ROW + row) * 8 + iota(at, 0) == iota(at, 1)
    labels = jnp.where(same, 1.0, -1.0).astype(F32)

    def weigh(mine, others):
        logits = scale * lax.dot_general(mine, others, (((1,), (1,)), ((), ())), preferred_element_type=F32) + shift
        weights = (-factor * labels * jax.nn.sigmoid(-labels * logits)).astype(BF16)
        return jnp.dot(weights, others, preferred_element_type=F32)

    embed_grad = weigh(embed_b, n.everyone[...].reshape(batch, width))
    pooled_grad = (embed_grad - embed * jnp.sum(embed * embed_grad, -1, keepdims=True)) / pooled_norm
    out_grad = pooled_grad * (1.0 / SEQ)
    n.own_grad[...] = out_grad
    grads.start(out_grad)
    grads.spread()
    grads.swap()
    grads.finish()

    def through_down(q):
        block = n.grads[q // 2, pl.ds((q % 2) * 4, 4)].reshape(-1, width)
        for x in range(EXP_DEV):
            back = lax.dot_general(block, n.w_down[x], (((1,), (1,)), ((), ())), preferred_element_type=F32)
            n.acc[x, pl.ds(q * 4, 4)] = back.reshape(4, N_ROW, 8, units)

    def deltas(r):
        n.q[r] = jnp.zeros(n.q.shape[1:], F32)

        def one(x):
            back = n.acc[x, :, r].reshape(records, units).astype(BF16)
            hidden_grad = jnp.dot(n.turned[r, x], back, preferred_element_type=F32)
            shape = (N_COL, capacity, units)
            hidden = n.hidden[x, :, r].reshape(slots, units).astype(F32)
            q = jnp.sum(hidden * hidden_grad, -1, keepdims=True)
            at = (slots, 128)
            q = jnp.where(iota(at, 1) == x * capacity + iota(at, 0) % capacity, q, 0.0)
            n.q[r] += jnp.sum(q.reshape(N_COL, capacity, 128), 1)
            gate_delta = hidden_grad * n.for_gate[x, :, r].reshape(slots, units).astype(F32)
            up_delta = hidden_grad * n.for_up[x, :, r].reshape(slots, units).astype(F32)
            n.for_gate[x, :, r] = gate_delta.astype(BF16).reshape(shape)
            n.for_up[x, :, r] = up_delta.astype(BF16).reshape(shape)
        loop(0, EXP_DEV, one)

    def backward(r):
        def one(x):
            total = fast(n.for_gate[x, :, r].reshape(slots, units), n.w_gate[x], ((1,), (1,)))
            total = total + fast(n.for_up[x, :, r].reshape(slots, units), n.w_up[x], ((1,), (1,)))
            n.back[x, :, r] = total.astype(BF16).reshape(N_COL, capacity, width)
        loop(0, EXP_DEV, one)

    def target(d, at_row):
        return n.back.at[:, (place + d) % N_COL, at_row]

    def far_back(rel, d):
        src = target(d, row_of(rel, 2))
        return remote(src, n.far_buf.at[rel, d], n.bf_send.at[rel, d], n.bf_recv.at[rel, d], row_of(0, near_of(d % 2)), col)

    def near_back(way, rel, d):
        src = target(d, row_of(rel, near_of(way)))
        return remote(
            src, n.near_buf.at[way, rel, d], n.bn_send.at[way, rel, d], n.bn_recv.at[way, rel, d],
            row_of(0, near_of(way)), col,
        )

    def from_across(step, d):
        if step == 0:
            return n.x_buf.at[d]
        return n.x_last.at[step % 4 - 1, d - X_BACK]

    def across_back(step, d):
        return remote(
            target(d, row_of(1, step)), from_across(step, d), n.bx_send.at[step % 4, d], n.bx_recv.at[step % 4, d],
            other_row, col,
        )

    def add_into(place_of_sum, *terms):
        for x in range(EXP_DEV):
            total = place_of_sum[x].astype(F32)
            for term in terms:
                total = total + term[x].astype(F32)
            place_of_sum[x] = total.astype(BF16)

    def q_row(d):
        to = (row + d) % N_ROW
        return remote(n.q.at[to], n.q_buf.at[d - 1], n.q1_send.at[d - 1], n.q1_recv.at[d - 1], to, col)

    embeds.spread()
    loop(0, 4, through_down)
    deltas(row_of(1, 2))
    backward(row_of(1, 2))
    loop(0, X_BACK, lambda d: far_back(1, d).start())
    loop(X_BACK, N_COL, lambda d: across_back(2, d).start())

    def other_deltas(i):
        r = row_of(1, 2)
        deltas((r + i) % N_ROW)

    loop(1, N_ROW, other_deltas)
    begin(N_ROW, q_row)
    loop(0, 2, lambda way: backward(row_of(1, near_of(way))))
    loop(0, X_BACK, lambda d: near_back(1 - d % 2, 1, d).start())
    loop(X_BACK, N_COL, lambda d: (across_back(1, d).start(), across_back(-1, d).start()))
    backward(row_of(0, 2))
    loop(0, X_BACK, lambda d: far_back(0, d).start())

    def far_first(d):
        across_back(2, d).wait_recv()
        add_into(target(d, row_of(0, 2)), from_across(2, d))
        far_back(0, d).start()

    loop(X_BACK, N_COL, far_first)
    loop(1, N_ROW, lambda d: q_row(d).wait_recv())
    total = n.q[row]
    for d in range(N_ROW - 1):
        total = total + n.q_buf[d]
    n.q_msg[...] = jnp.broadcast_to(total[:, None, :], n.q_msg.shape)
    n.q_in[place] = n.q_msg[place]

    def q_col(d):
        to = (place + d) % N_COL
        return remote(n.q_msg.at[to], n.q_in.at[place], n.q2_send.at[d - 1], n.q2_recv.at[d - 1], row, column_of(to))

    begin(N_COL, q_col)
    embeds.relay()
    loop(0, 2, lambda way: backward(row_of(0, near_of(way))))
    loop(0, X_BACK, lambda d: near_back(1 - d % 2, 0, d).start())
    backward(other_row)
    loop(X_BACK, N_COL, lambda d: across_back(0, d).start())
    backward(row)

    def far_added(rel, d):
        way = d % 2
        far_back(rel, d).wait_recv()
        add_into(target(d, row_of(rel, near_of(way))), n.far_buf.at[rel, d])
        near_back(way, rel, d).start()

    def near_first(d):
        for step in (1, -1):
            across_back(step, d).wait_recv()
            add_into(target(d, row_of(0, step)), from_across(step, d))
        near_back(1 - d % 2, 0, d).start()

    loop(0, X_BACK, lambda d: far_added(1, d))
    loop(X_BACK, N_COL, near_first)
    loop(X_BACK, N_COL, lambda d: far_added(0, d))
    loop(0, X_BACK, lambda d: far_added(0, d))
    embeds.swap()

    def weight_grads(x):
        dims = (((0,), (0,)), ((), ()))

        def one(t):
            at = pl.ds(pl.multiple_of(t * 256, 256), 256)
            rows = n.grid[x, :, :, :, at].reshape(-1, 256)
            n.d_gate[x, at] = lax.dot_general(
                rows, n.for_gate[x].reshape(-1, units), dims, preferred_element_type=F32
            )
            n.d_up[x, at] = lax.dot_general(
                rows, n.for_up[x].reshape(-1, units), dims, preferred_element_type=F32
            )
        loop(0, width // 256, one)

    loop(1, N_COL, lambda d: arrived(n.q_in.at[(place + N_COL - d) % N_COL], n.q2_recv.at[d - 1]))
    found = []
    for k in range(2):
        lines = exact(one_hot(to_place[k], N_COL), n.q_in[:, 0, :], ((1,), (0,)))
        found.append(jnp.sum(one_hot(in_line[k], 128) * lines, -1, keepdims=True))
    both = found[0] + found[1]
    score_grad = jnp.zeros((tok_count, 128), F32)
    for k in range(2):
        score_grad = score_grad + one_hot(ids[k], 128) * (found[k] - gates[k] * both)
    router_part = exact(score_grad.T[:experts], norm_in.astype(F32), ((1,), (0,)))
    n.dr[...] = jnp.zeros(n.dr.shape, F32)
    tiles = width // 128
    n.router_term[...] = exact(score_grad[:, :experts], n.router[...], ((1,), (0,)))
    for k in range(experts // 8 * tiles):
        i, j = k // tiles, k % tiles
        n.dr[k // 2, k % 2] = router_part[i * 8 : i * 8 + 8, j * 128 : (j + 1) * 128]

    def scatter(d):
        to = (col + d) % N_COL
        return remote(n.dr.at[to], n.dr_in.at[col], n.d1_send.at[d - 1], n.d1_recv.at[d - 1], row, to)

    def tell_row(d):
        at = n.dr_sum.at[row]
        return remote(at, at, n.d2_send.at[d - 1], n.d2_recv.at[d - 1], (row + d) % N_ROW, col)

    def tell_col(d):
        at = n.dr_out.at[col]
        return remote(at, at, n.d3_send.at[d - 1], n.d3_recv.at[d - 1], row, (col + d) % N_COL)

    begin(N_COL, scatter)
    n.dr_in[col] = n.dr[col]
    weight_grads(0)

    def crossed(d):
        near_back(0, 1, d).wait_recv()
        near_back(1, 1, d).wait_recv()
        add_into(target(d, other_row), n.near_buf.at[0, 1, d], n.near_buf.at[1, 1, d])
        across_back(0, d).start()

    loop(0, X_BACK, crossed)
    loop(1, N_COL, lambda d: arrived(n.dr_in.at[(col + N_COL - d) % N_COL], n.d1_recv.at[d - 1]))
    n.dr_sum[row] = jnp.sum(n.dr_in[...], 0)
    begin(N_ROW, tell_row)
    weight_grads(1)

    def down_grads(x):
        def one(t):
            at = pl.ds(pl.multiple_of(t * 128, 128), 128)
            n.d_down[x, at] = fast(
                n.hb[x, :, :, at].reshape(-1, 128), n.grads[...].reshape(batch, width), ((0,), (0,))
            )
        loop(0, units // 128, one)

    def home(d):
        return remote(
            target(d, row), n.slots.at[place], n.h_send.at[d], n.h_recv.at[d], row, column_of((place + d) % N_COL)
        )

    own_home = pltpu.make_async_copy(target(0, row), n.slots.at[place], n.own_sem)

    def complete(d):
        near_back(0, 0, d).wait_recv()
        near_back(1, 0, d).wait_recv()
        across_back(0, d).wait_recv()
        add_into(target(d, row), n.near_buf.at[0, 0, d], n.near_buf.at[1, 0, d], from_across(0, d))

        @pl.when(d != 0)
        def _():
            home(d).start()

        @pl.when(d == 0)
        def _():
            own_home.start()

    loop(X_BACK, N_COL, complete)
    loop(1, N_ROW, lambda d: arrived(n.dr_sum.at[(row + N_ROW - d) % N_ROW], n.d2_recv.at[d - 1]))
    n.dr_out[col] = jnp.sum(n.dr_sum[...], 0)
    begin(N_COL, tell_col)
    down_grads(0)
    down_grads(1)
    embeds.finish()
    text_grad = weigh(text_unit.astype(BF16), n.e_whole[...].reshape(batch, width))
    n.d_text[...] = (text_grad - text_unit * jnp.sum(text_unit * text_grad, -1, keepdims=True)) / text_norm
    loop(0, X_BACK, complete)

    def back_first(d):
        far_back(1, d).wait_send()
        for way in range(2):
            near_back(way, 1, d).wait_send()

    def back_all(d):
        far_back(0, d).wait_send()
        across_back(0, d).wait_send()
        for way in range(2):
            near_back(way, 0, d).wait_send()

    def back_last(d):
        for step in (-1, 1, 2):
            across_back(step, d).wait_send()

    pending.append(lambda: loop(0, X_BACK, back_first))
    pending.append(lambda: loop(0, N_COL, back_all))
    pending.append(lambda: loop(X_BACK, N_COL, back_last))
    pending.append(lambda: loop(1, N_COL, lambda d: home(d).wait_send()))

    loop(1, N_COL, lambda d: arrived(n.dr_out.at[(col + N_COL - d) % N_COL], n.d3_recv.at[d - 1]))
    for wait in pending:
        wait()
    loop(1, N_COL, lambda d: arrived(n.slots.at[source(d)], n.h_recv.at[d]))
    own_home.wait()
    for k in range(experts // 8 * tiles):
        i, j = k // tiles, k % tiles
        n.d_router[i * 8 : i * 8 + 8, j * 128 : (j + 1) * 128] = n.dr_out[k // 2, k % 2]
    input_sum = fast(hit, n.slots[...].reshape(-1, width), ((1,), (0,)))
    norm_grad = input_sum + n.router_term[...]
    normed = n.tokens[...].astype(F32) * inverse_rms
    out_grad = jnp.broadcast_to(n.own_grad[...][:, None, :], (8, SEQ, width)).reshape(tok_count, width)
    n.d_tokens[...] = out_grad + inverse_rms * (
        norm_grad - normed * jnp.mean(norm_grad * normed, -1, keepdims=True)
    )


def fused(ins):
    tok_count, width = ins["tokens"].shape
    units = ins["w_gate"].shape[-1]
    experts = EXP_DEV * N_COL
    capacity = max(2, 4 * tok_count // experts)
    slots, records = N_COL * capacity, N_COL * 8
    whole = (2, N_XZ, N_ROW * 8, width)
    block = (EXP_DEV, capacity, width)
    grid = (EXP_DEV, N_COL, N_ROW, capacity)
    outs = {
        "d_text": ((8, width), F32, VMEM),
        "d_tokens": ((tok_count, width), F32, VMEM),
        "d_gate": (ins["w_gate"].shape, F32, VMEM),
        "d_up": (ins["w_up"].shape, F32, VMEM),
        "d_down": (ins["w_down"].shape, F32, VMEM),
        "d_router": (ins["router"].shape, F32, VMEM),
    }
    scratch = {
        "rows": ((N_COL, EXP_DEV, capacity, width), BF16),
        "meta": ((N_COL, 8, 128), F32),
        "own_grad": ((8, width), F32),
        "router_term": ((tok_count, width), F32),
        "slots": ((N_COL, EXP_DEV, capacity, width), BF16),
        "dr_out": ((N_COL, 2, 8, 128), F32),
        "grid": (grid + (width,), BF16),
        "table": ((N_COL, 8, 128), F32),
        "compact": ((N_ROW, N_COL // 4, 8, 128), F32),
        "t_stage": ((N_ROW, 8, width), F32),
        "everyone": ((2, 2, 4) + whole[2:], BF16),
        "turned": ((N_ROW, EXP_DEV, slots, records), BF16),
        "hidden": (grid + (units,), BF16),
        "for_gate": (grid + (units,), BF16),
        "for_up": (grid + (units,), BF16),
        "acc": ((EXP_DEV, N_COL, N_ROW, 8, units), F32),
        "hb": ((EXP_DEV, 4, N_ROW * records // 4, units), BF16),
        "sums_row": ((N_ROW, 8, width), F32),
        "from_row": ((N_ROW - 1, 8, width), F32),
        "e_stage": ((N_ROW, 8, width), F32),
        "e_whole": ((2, 2, 4) + whole[2:], BF16),
        "g_stage": ((N_ROW, 8, width), F32),
        "grads": (whole, BF16),
        "back": (grid + (width,), BF16),
        "far_buf": ((2, N_COL) + block, BF16),
        "near_buf": ((2, 2, N_COL) + block, BF16),
        "x_buf": ((N_COL,) + block, BF16),
        "x_last": ((3, N_COL - X_BACK) + block, BF16),
        "q": ((N_ROW, N_COL, 128), F32),
        "q_buf": ((N_ROW - 1, N_COL, 128), F32),
        "q_msg": ((N_COL, 8, 128), F32),
        "q_in": ((N_COL, 8, 128), F32),
        "dr": ((N_COL, 2, 8, 128), F32),
        "dr_in": ((N_COL, 2, 8, 128), F32),
        "dr_sum": ((N_ROW, 2, 8, 128), F32),
    }
    row, col, chips = (N_ROW - 1,), (N_COL - 1,), (N_XZ - 1,)
    sems = {
        "own_sem": (),
        "m_send": col, "m_recv": col, "a_send": col, "a_recv": (N_COL,), "c_send": row, "c_recv": row,
        "x_send": (4, N_COL), "x_recv": (4, N_COL), "n_send": (2, 2, N_COL), "n_recv": (2, 2, N_COL),
        "f_send": (2, N_COL), "f_recv": (2, N_COL),
        "s1": (), "r1": (), "s2": chips, "r2": chips, "s3": row, "r3": row,
        "bf_send": (2, N_COL), "bf_recv": (2, N_COL), "bn_send": (2, 2, N_COL), "bn_recv": (2, 2, N_COL),
        "bx_send": (4, N_COL), "bx_recv": (4, N_COL), "h_send": (N_COL,), "h_recv": (N_COL,),
        "q1_send": row, "q1_recv": row, "q2_send": col, "q2_recv": col,
        "d1_send": col, "d1_recv": col, "d2_send": row, "d2_recv": row, "d3_send": col, "d3_recv": col,
    }
    for letter in "teg":
        for kind in "sr":
            sems.update({letter + kind + "1": row, letter + kind + "2": chips, letter + kind + "3": (N_XZ,), letter + kind + "4": ()})
    names = list(ins) + list(outs) + list(scratch) + list(sems)
    result = pl.pallas_call(
        functools.partial(fused_kernel, names),
        out_shape=tuple(
            pltpu.VMEM(shape, dtype) if name in KEPT else jax.ShapeDtypeStruct(shape, dtype)
            for name, (shape, dtype, _) in outs.items()
        ),
        in_specs=[SMEM if name in ("log_scale", "bias", "loss_scale") else VMEM for name in ins],
        out_specs=tuple(spec for _, _, spec in outs.values()),
        scratch_shapes=[pltpu.VMEM(shape, dtype) for shape, dtype in scratch.values()]
        + [pltpu.SemaphoreType.DMA(shape) for shape in sems.values()],
        compiler_params=pltpu.CompilerParams(
            collective_id=0, has_side_effects=True, vmem_limit_bytes=50 << 20
        ),
    )(*ins.values())
    return result


def body(tokens, expert_ids, text, w_gate, w_up, w_down, router, log_scale, bias, loss_scale):
    *grads, d_router = fused({
        "tokens": tokens, "ids": expert_ids.T, "text": text, "w_gate": w_gate, "w_up": w_up, "w_down": w_down,
        "router": router.T, "log_scale": log_scale, "bias": bias, "loss_scale": loss_scale,
    })
    return (*grads, d_router.T)


def solution(mesh):
    in_specs = (
        P(("row", "col"), None),
        P(("row", "col"), None),
        P(("row", "col"), None),
        P("col", None, "row"),
        P("col", None, "row"),
        P("col", "row", None),
        P(),
        P(),
        P(),
        P(),
    )
    out_specs = (
        P(("row", "col"), None),
        P(("row", "col"), None),
        P("col", None, "row"),
        P("col", None, "row"),
        P("col", "row", None),
        P(),
    )
    return jax.shard_map(body, mesh=mesh, in_specs=in_specs, out_specs=out_specs, check_vma=False)
```

time: 220 us -> 191 us (0.87)
  Pallas kernels: 201 us -> 182 us
  local copies, waits for them, and re-layouts: 15.4 us -> 6.21 us
    pallas_call x1, Pallas kernels: 201 us -> 182 us  [fused(): pl.pallas_call(functools.partial(fused_kernel, names), out_shape=tuple((p...]
    unnamed x11 -> x6, local copies, waits for them, and re-layouts: 13.6 us -> 6.21 us
where the time goes in v3:
time: 191 us
  Pallas kernels  182 us (95%)
  local copies, waits for them, and re-layouts  6.21 us (3%)
  between operations  2.58 us (1%)
    pallas_call x1, Pallas kernels, fused(): pl.pallas_call(functools.partial(fused_kernel, names), out_shape=tuple((p...  182 us
    unnamed x6, local copies, waits for them, and re-layouts  6.21 us

profile of v3, /device:TPU:1, one launch (start us, length us, event | category | flops | bytes accessed | tf_op | source)
XLA Modules:
  0.0 191.1 jit_solution(2341139259807435449)
XLA Ops:
  2.6 182.3 %shard_map.145 = (f32[8,768]{1,0:T(8,128)S(1)}, f32[128,768]{1,0:T(8,128)S(1)}, f32[2,768,384]{2,1,0:T(8,128)S(1)}, f32[2,768,384]{2,1,0:T(8,128)S(1)}, f32[2,38...) custom-call(bf16[128,768]{1,0:T(8,128)(2,1)} %refs_0_.1, s32[2,128]{1,0:T(2,128)} %bitcast.5, bf16[8,768]{1,0:T(8,128)(2,1)} %refs_2_.1, ...), custom_call_target="tpu_custom_call" | custom-call | tf_op jit(solution)/shard_map/pallas_call | solution.py:845
  184.9 0.6 copy.22
  185.5 0.6 copy.27
  186.1 0.7 copy.23
  186.9 1.4 copy.24
  188.3 1.4 copy.25
  189.7 1.4 copy.26

commit v4 on v3

--- a/solution.py
+++ b/solution.py
@@ -17,7 +17,7 @@
 SMEM = pl.BlockSpec(memory_space=pltpu.SMEM)
 ANY = pl.BlockSpec(memory_space=pl.ANY)
 N_ROW, N_COL, N_XZ = 8, 16, 8
-X_OUT, X_BACK = 9, 8
+X_OUT, X_BACK = 10, 9
 KEPT = ("d_gate", "d_up", "d_down", "d_text", "d_tokens", "d_router")
 
 
@@ -220,6 +220,12 @@
     def one_hot(at, lanes):
         return (iota((at.shape[0], lanes), 1) == at).astype(F32)
 
+    def fetch(k):
+        source, target = ((n.in_gate, n.w_gate), (n.in_up, n.w_up), (n.in_down, n.w_down))[k]
+        return pltpu.make_async_copy(source, target, n.w_sem.at[k])
+
+    for k in range(3):
+        fetch(k).start()
     greeted = greet(True, True)
 
     tokens = n.tokens[...].astype(F32)
@@ -356,6 +362,8 @@
 
     own.wait()
     loop(0, N_COL, from_column)
+    for k in range(3):
+        fetch(k).wait()
     texts.spread()
     forward(row)
     loop(1, N_ROW, lambda d: arrived(n.compact.at[(row + N_ROW - d) % N_ROW], n.c_recv.at[d - 1]))
@@ -389,20 +397,20 @@
         got_across(-1, d)
         got_across(1, d)
 
-    loop(0, X_OUT, x_first)
+    loop(0, N_COL - X_OUT, y_first)
+    loop(N_COL - X_OUT, N_COL, x_first)
     texts.relay()
-    loop(X_OUT, N_COL, y_first)
     loop(0, 2, lambda way: forward(row_of(0, near_of(way))))
-    loop(X_OUT, N_COL, y_first_far)
+    loop(0, N_COL - X_OUT, y_first_far)
     forward(other_row)
     texts.swap()
-    loop(0, X_OUT, x_first_other)
-    loop(X_OUT, N_COL, y_first_other)
+    loop(N_COL - X_OUT, N_COL, x_first_other)
+    loop(0, N_COL - X_OUT, y_first_other)
     loop(0, 2, lambda way: forward(row_of(1, near_of(way))))
-    loop(0, X_OUT, lambda d: got_far(0, d))
+    loop(N_COL - X_OUT, N_COL, lambda d: got_far(0, d))
     forward(row_of(0, 2))
-    loop(0, X_OUT, lambda d: got_far(1, d))
-    loop(X_OUT, N_COL, lambda d: got_across(2, d))
+    loop(N_COL - X_OUT, N_COL, lambda d: got_far(1, d))
+    loop(0, N_COL - X_OUT, lambda d: got_across(2, d))
     forward(row_of(1, 2))
 
     def sent_first(d):
@@ -420,9 +428,9 @@
         for step in (-1, 1, 2):
             across(step, d).wait_send()
 
-    pending.append(lambda: loop(0, X_OUT, sent_first))
+    pending.append(lambda: loop(N_COL - X_OUT, N_COL, sent_first))
     pending.append(lambda: loop(0, N_COL, sent_all))
-    pending.append(lambda: loop(X_OUT, N_COL, sent_last))
+    pending.append(lambda: loop(0, N_COL - X_OUT, sent_last))
 
     def quarter(q):
         return n.hb[0, q], n.hb[1, q]
@@ -555,7 +563,7 @@
     def from_across(step, d):
         if step == 0:
             return n.x_buf.at[d]
-        return n.x_last.at[step % 4 - 1, d - X_BACK]
+        return n.x_last.at[step % 4 - 1, d]
 
     def across_back(step, d):
         return remote(
@@ -578,8 +586,8 @@
     loop(0, 4, through_down)
     deltas(row_of(1, 2))
     backward(row_of(1, 2))
-    loop(0, X_BACK, lambda d: far_back(1, d).start())
-    loop(X_BACK, N_COL, lambda d: across_back(2, d).start())
+    loop(N_COL - X_BACK, N_COL, lambda d: far_back(1, d).start())
+    loop(0, N_COL - X_BACK, lambda d: across_back(2, d).start())
 
     def other_deltas(i):
         r = row_of(1, 2)
@@ -588,17 +596,17 @@
     loop(1, N_ROW, other_deltas)
     begin(N_ROW, q_row)
     loop(0, 2, lambda way: backward(row_of(1, near_of(way))))
-    loop(0, X_BACK, lambda d: near_back(1 - d % 2, 1, d).start())
-    loop(X_BACK, N_COL, lambda d: (across_back(1, d).start(), across_back(-1, d).start()))
+    loop(N_COL - X_BACK, N_COL, lambda d: near_back(1 - d % 2, 1, d).start())
+    loop(0, N_COL - X_BACK, lambda d: (across_back(1, d).start(), across_back(-1, d).start()))
     backward(row_of(0, 2))
-    loop(0, X_BACK, lambda d: far_back(0, d).start())
+    loop(N_COL - X_BACK, N_COL, lambda d: far_back(0, d).start())
 
     def far_first(d):
         across_back(2, d).wait_recv()
         add_into(target(d, row_of(0, 2)), from_across(2, d))
         far_back(0, d).start()
 
-    loop(X_BACK, N_COL, far_first)
+    loop(0, N_COL - X_BACK, far_first)
     loop(1, N_ROW, lambda d: q_row(d).wait_recv())
     total = n.q[row]
     for d in range(N_ROW - 1):
@@ -613,9 +621,9 @@
     begin(N_COL, q_col)
     embeds.relay()
     loop(0, 2, lambda way: backward(row_of(0, near_of(way))))
-    loop(0, X_BACK, lambda d: near_back(1 - d % 2, 0, d).start())
+    loop(N_COL - X_BACK, N_COL, lambda d: near_back(1 - d % 2, 0, d).start())
     backward(other_row)
-    loop(X_BACK, N_COL, lambda d: across_back(0, d).start())
+    loop(0, N_COL - X_BACK, lambda d: across_back(0, d).start())
     backward(row)
 
     def far_added(rel, d):
@@ -630,10 +638,10 @@
             add_into(target(d, row_of(0, step)), from_across(step, d))
         near_back(1 - d % 2, 0, d).start()
 
-    loop(0, X_BACK, lambda d: far_added(1, d))
-    loop(X_BACK, N_COL, near_first)
-    loop(X_BACK, N_COL, lambda d: far_added(0, d))
-    loop(0, X_BACK, lambda d: far_added(0, d))
+    loop(N_COL - X_BACK, N_COL, lambda d: far_added(1, d))
+    loop(0, N_COL - X_BACK, near_first)
+    loop(0, N_COL - X_BACK, lambda d: far_added(0, d))
+    loop(N_COL - X_BACK, N_COL, lambda d: far_added(0, d))
     embeds.swap()
 
     def weight_grads(x):
@@ -689,7 +697,7 @@
         add_into(target(d, other_row), n.near_buf.at[0, 1, d], n.near_buf.at[1, 1, d])
         across_back(0, d).start()
 
-    loop(0, X_BACK, crossed)
+    loop(N_COL - X_BACK, N_COL, crossed)
     loop(1, N_COL, lambda d: arrived(n.dr_in.at[(col + N_COL - d) % N_COL], n.d1_recv.at[d - 1]))
     n.dr_sum[row] = jnp.sum(n.dr_in[...], 0)
     begin(N_ROW, tell_row)
@@ -724,7 +732,7 @@
         def _():
             own_home.start()
 
-    loop(X_BACK, N_COL, complete)
+    loop(0, N_COL - X_BACK, complete)
     loop(1, N_ROW, lambda d: arrived(n.dr_sum.at[(row + N_ROW - d) % N_ROW], n.d2_recv.at[d - 1]))
     n.dr_out[col] = jnp.sum(n.dr_sum[...], 0)
     begin(N_COL, tell_col)
@@ -733,7 +741,7 @@
     embeds.finish()
     text_grad = weigh(text_unit.astype(BF16), n.e_whole[...].reshape(batch, width))
     n.d_text[...] = (text_grad - text_unit * jnp.sum(text_unit * text_grad, -1, keepdims=True)) / text_norm
-    loop(0, X_BACK, complete)
+    loop(N_COL - X_BACK, N_COL, complete)
 
     def back_first(d):
         far_back(1, d).wait_send()
@@ -750,9 +758,9 @@
         for step in (-1, 1, 2):
             across_back(step, d).wait_send()
 
-    pending.append(lambda: loop(0, X_BACK, back_first))
+    pending.append(lambda: loop(N_COL - X_BACK, N_COL, back_first))
     pending.append(lambda: loop(0, N_COL, back_all))
-    pending.append(lambda: loop(X_BACK, N_COL, back_last))
+    pending.append(lambda: loop(0, N_COL - X_BACK, back_last))
     pending.append(lambda: loop(1, N_COL, lambda d: home(d).wait_send()))
 
     loop(1, N_COL, lambda d: arrived(n.dr_out.at[(col + N_COL - d) % N_COL], n.d3_recv.at[d - 1]))
@@ -774,7 +782,7 @@
 
 def fused(ins):
     tok_count, width = ins["tokens"].shape
-    units = ins["w_gate"].shape[-1]
+    units = ins["in_gate"].shape[-1]
     experts = EXP_DEV * N_COL
     capacity = max(2, 4 * tok_count // experts)
     slots, records = N_COL * capacity, N_COL * 8
@@ -784,12 +792,15 @@
     outs = {
         "d_text": ((8, width), F32, VMEM),
         "d_tokens": ((tok_count, width), F32, VMEM),
-        "d_gate": (ins["w_gate"].shape, F32, VMEM),
-        "d_up": (ins["w_up"].shape, F32, VMEM),
-        "d_down": (ins["w_down"].shape, F32, VMEM),
+        "d_gate": (ins["in_gate"].shape, F32, VMEM),
+        "d_up": (ins["in_up"].shape, F32, VMEM),
+        "d_down": (ins["in_down"].shape, F32, VMEM),
         "d_router": (ins["router"].shape, F32, VMEM),
     }
     scratch = {
+        "w_gate": (ins["in_gate"].shape, BF16),
+        "w_up": (ins["in_up"].shape, BF16),
+        "w_down": (ins["in_down"].shape, BF16),
         "rows": ((N_COL, EXP_DEV, capacity, width), BF16),
         "meta": ((N_COL, 8, 128), F32),
         "own_grad": ((8, width), F32),
@@ -828,7 +839,7 @@
     }
     row, col, chips = (N_ROW - 1,), (N_COL - 1,), (N_XZ - 1,)
     sems = {
-        "own_sem": (),
+        "own_sem": (), "w_sem": (3,),
         "m_send": col, "m_recv": col, "a_send": col, "a_recv": (N_COL,), "c_send": row, "c_recv": row,
         "x_send": (4, N_COL), "x_recv": (4, N_COL), "n_send": (2, 2, N_COL), "n_recv": (2, 2, N_COL),
         "f_send": (2, N_COL), "f_recv": (2, N_COL),
@@ -848,7 +859,10 @@
             pltpu.VMEM(shape, dtype) if name in KEPT else jax.ShapeDtypeStruct(shape, dtype)
             for name, (shape, dtype, _) in outs.items()
         ),
-        in_specs=[SMEM if name in ("log_scale", "bias", "loss_scale") else VMEM for name in ins],
+        in_specs=[
+            SMEM if name in ("log_scale", "bias", "loss_scale") else ANY if name.startswith("in_") else VMEM
+            for name in ins
+        ],
         out_specs=tuple(spec for _, _, spec in outs.values()),
         scratch_shapes=[pltpu.VMEM(shape, dtype) for shape, dtype in scratch.values()]
         + [pltpu.SemaphoreType.DMA(shape) for shape in sems.values()],
@@ -861,7 +875,7 @@
 
 def body(tokens, expert_ids, text, w_gate, w_up, w_down, router, log_scale, bias, loss_scale):
     *grads, d_router = fused({
-        "tokens": tokens, "ids": expert_ids.T, "text": text, "w_gate": w_gate, "w_up": w_up, "w_down": w_down,
+        "tokens": tokens, "ids": expert_ids.T, "text": text, "in_gate": w_gate, "in_up": w_up, "in_down": w_down,
         "router": router.T, "log_scale": log_scale, "bias": bias, "loss_scale": loss_scale,
     })
     return (*grads, d_router.T)

time: 191 us -> 183 us (0.958)
  Pallas kernels: 182 us -> 174 us
    pallas_call x1, Pallas kernels: 182 us -> 174 us  [fused(): pl.pallas_call(functools.partial(fused_kernel, names), out_shape=tuple((p...]
where the time goes in v4:
time: 183 us; the launch traced here: 182 us
  Pallas kernels  174 us (95%)
  local copies, waits for them, and re-layouts  6.21 us (3%)
  between operations  2.58 us (1%)
    pallas_call x1, Pallas kernels, fused(): pl.pallas_call(functools.partial(fused_kernel, names), out_shape=tuple((p...  174 us
    unnamed x6, local copies, waits for them, and re-layouts  6.21 us

profile of v4, /device:TPU:1, one launch (start us, length us, event | category | flops | bytes accessed | tf_op | source)
XLA Modules:
  0.0 182.4 jit_solution(2052710078619963442)
XLA Ops:
  2.6 173.6 %shard_map.145 = (f32[8,768]{1,0:T(8,128)S(1)}, f32[128,768]{1,0:T(8,128)S(1)}, f32[2,768,384]{2,1,0:T(8,128)S(1)}, f32[2,768,384]{2,1,0:T(8,128)S(1)}, f32[2,38...) custom-call(bf16[128,768]{1,0:T(8,128)(2,1)} %refs_0_.1, s32[2,128]{1,0:T(2,128)} %bitcast.5, bf16[8,768]{1,0:T(8,128)(2,1)} %refs_2_.1, ...), custom_call_target="tpu_custom_call" | custom-call | tf_op jit(solution)/shard_map/pallas_call | solution.py:856
  176.2 0.6 copy.22
  176.8 0.6 copy.27
  177.4 0.7 copy.23
  178.2 1.4 copy.24
  179.6 1.4 copy.25
  181.0 1.4 copy.26

commit v5 on v4

--- a/solution.py
+++ b/solution.py
@@ -619,12 +619,12 @@
         return remote(n.q_msg.at[to], n.q_in.at[place], n.q2_send.at[d - 1], n.q2_recv.at[d - 1], row, column_of(to))
 
     begin(N_COL, q_col)
-    embeds.relay()
     loop(0, 2, lambda way: backward(row_of(0, near_of(way))))
     loop(N_COL - X_BACK, N_COL, lambda d: near_back(1 - d % 2, 0, d).start())
     backward(other_row)
     loop(0, N_COL - X_BACK, lambda d: across_back(0, d).start())
     backward(row)
+    embeds.relay()
 
     def far_added(rel, d):
         way = d % 2
@@ -689,7 +689,6 @@
 
     begin(N_COL, scatter)
     n.dr_in[col] = n.dr[col]
-    weight_grads(0)
 
     def crossed(d):
         near_back(0, 1, d).wait_recv()
@@ -701,6 +700,7 @@
     loop(1, N_COL, lambda d: arrived(n.dr_in.at[(col + N_COL - d) % N_COL], n.d1_recv.at[d - 1]))
     n.dr_sum[row] = jnp.sum(n.dr_in[...], 0)
     begin(N_ROW, tell_row)
+    weight_grads(0)
     weight_grads(1)
 
     def down_grads(x):

time: 183 us -> 183 us (level)
  no operation moved by 1% of the time
where the time goes in v5:
time: 183 us
  Pallas kernels  174 us (95%)
  local copies, waits for them, and re-layouts  6.21 us (3%)
  between operations  2.58 us (1%)
    pallas_call x1, Pallas kernels, fused(): pl.pallas_call(functools.partial(fused_kernel, names), out_shape=tuple((p...  174 us
    unnamed x6, local copies, waits for them, and re-layouts  6.21 us

profile of v5, /device:TPU:1, one launch (start us, length us, event | category | flops | bytes accessed | tf_op | source)
XLA Modules:
  0.0 182.6 jit_solution(8771489112120387416)
XLA Ops:
  2.6 173.8 %shard_map.145 = (f32[8,768]{1,0:T(8,128)S(1)}, f32[128,768]{1,0:T(8,128)S(1)}, f32[2,768,384]{2,1,0:T(8,128)S(1)}, f32[2,768,384]{2,1,0:T(8,128)S(1)}, f32[2,38...) custom-call(bf16[128,768]{1,0:T(8,128)(2,1)} %refs_0_.1, s32[2,128]{1,0:T(2,128)} %bitcast.5, bf16[8,768]{1,0:T(8,128)(2,1)} %refs_2_.1, ...), custom_call_target="tpu_custom_call" | custom-call | tf_op jit(solution)/shard_map/pallas_call | solution.py:856
  176.4 0.6 copy.22
  177.0 0.6 copy.27
  177.7 0.7 copy.23
  178.4 1.4 copy.24
  179.8 1.4 copy.25
  181.2 1.4 copy.26
